TPU v7x, 128 devices: a whole 4x4x4 slice. The times are simulated.
128 devices in a mesh: expert: 32 (over y, x, core), dp: 4 (over z).
Axes of the slice: x: 4, y: 4, z: 4, core: 2. Of those that a mesh axis runs over, the one named last changes fastest.
Arguments:
- tokens: bfloat16 [16384, 2048], P(('expert', 'dp')), may hold values from -6 to 6
- expert_ids: int32 [16384, 8], P(('expert', 'dp')), may hold values from 0 to 63, all different within a row; in each aligned block of 128 rows (0 to 127, 128 to 255, ...) at most 24 rows name the same one
- gate_prob: float32 [16384, 8], P(('expert', 'dp')), may hold values from 0.05 to 0.3
- w_gate: bfloat16 [64, 2048, 384], P('expert', 'dp'), may hold values from -0.125 to 0.125
- w_up: bfloat16 [64, 2048, 384], P('expert', 'dp'), may hold values from -0.125 to 0.125
- w_down: bfloat16 [64, 384, 2048], P('expert', None, 'dp'), may hold values from -0.3125 to 0.3125
- grad_out: bfloat16 [16384, 2048], P(('expert', 'dp')), may hold values from -6 to 6
Outputs:
- mixed: bfloat16 [16384, 2048], P(('expert', 'dp'))
- grad_tokens: bfloat16 [16384, 2048], P(('expert', 'dp'))
- grad_gate: bfloat16 [64, 2048, 384], P('expert', 'dp')
- grad_up: bfloat16 [64, 2048, 384], P('expert', 'dp')
- grad_down: bfloat16 [64, 384, 2048], P('expert', None, 'dp')
Inputs may be any that keep to these rules, and one draw needn't show every extreme that they name: `expert_ids`: each row names 8 different experts. In each aligned block of 128 rows (the rows of one device) no expert is named by more than 24 rows, a bound that some block reaches.
All inputs are finite; a program needn't handle non-finite values.
Results may differ from a plain program's by a relative error of at most 0.015.
Values may be sent and summed in bfloat16 or wider, within the bound.
A program may use at most 128 MiB of HBM per device.

v0:
```python
import jax
import jax.numpy as jnp
from jax import lax
from jax.sharding import PartitionSpec as P


def silu_grad(a):
    s = jax.nn.sigmoid(a)
    return s * (1.0 + a * (1.0 - s))


def per_device(tokens, expert_ids, gate_prob, w_gate, w_up, w_down, grad_out):
    rows, width = tokens.shape
    topk = expert_ids.shape[1]
    groups = lax.axis_size("expert")
    local = w_gate.shape[0]
    experts = local * groups
    cap = 3 * rows * topk // (2 * experts)
    flat = expert_ids.reshape(-1)
    onehot = (flat[:, None] == jnp.arange(experts, dtype=jnp.int32)[None, :]).astype(jnp.int32)
    before = jnp.cumsum(onehot, axis=0) - onehot
    slot = jnp.sum(before * onehot, axis=1)
    pos = flat * cap + slot
    pair_tok = jnp.repeat(jnp.arange(rows, dtype=jnp.int32), topk)
    send_x = jnp.zeros((experts * cap, width), jnp.bfloat16).at[pos].set(tokens[pair_tok])
    send_x = send_x.reshape(groups, local, cap, width)
    pair_grad = (gate_prob.reshape(-1, 1) * grad_out[pair_tok].astype(jnp.float32)).astype(
        jnp.bfloat16
    )
    send_g = jnp.zeros((experts * cap, width), jnp.bfloat16).at[pos].set(pair_grad)
    send_g = send_g.reshape(groups, local, cap, width)
    recv_x = lax.all_to_all(send_x, "expert", split_axis=0, concat_axis=2, tiled=True)
    x_in = recv_x.reshape(local, groups * cap, width)
    full_gate, full_up = (
        lax.all_gather(w_gate, "dp", axis=1, tiled=True),
        lax.all_gather(w_up, "dp", axis=1, tiled=True),
    )
    full_down = lax.all_gather(w_down, "dp", axis=2, tiled=True)
    a = jnp.einsum("lrm,lmf->lrf", x_in, full_gate, preferred_element_type=jnp.float32)
    b = jnp.einsum("lrm,lmf->lrf", x_in, full_up, preferred_element_type=jnp.float32)
    hidden = (jax.nn.silu(a) * b).astype(jnp.bfloat16)
    expert_out = jnp.einsum(
        "lrf,lfm->lrm", hidden, full_down, preferred_element_type=jnp.float32
    ).astype(jnp.bfloat16)
    back = lax.all_to_all(
        expert_out.reshape(1, local, groups * cap, width),
        "expert",
        split_axis=2,
        concat_axis=0,
        tiled=True,
    )
    picked = back.reshape(experts * cap, width)[pos].reshape(rows, topk, width)
    mixed = jnp.sum(gate_prob[:, :, None] * picked.astype(jnp.float32), axis=1).astype(jnp.bfloat16)
    recv_g = lax.all_to_all(send_g, "expert", split_axis=0, concat_axis=2, tiled=True)
    dy_in = recv_g.reshape(local, groups * cap, width)
    grad_hidden = jnp.einsum("lrm,lfm->lrf", dy_in, full_down, preferred_element_type=jnp.float32)
    grad_a = (grad_hidden * b * silu_grad(a)).astype(jnp.bfloat16)
    grad_b = (grad_hidden * jax.nn.silu(a)).astype(jnp.bfloat16)
    pair_dx = (
        jnp.einsum("lrf,lmf->lrm", grad_a, full_gate, preferred_element_type=jnp.float32)
        + jnp.einsum("lrf,lmf->lrm", grad_b, full_up, preferred_element_type=jnp.float32)
    ).astype(jnp.bfloat16)
    back_dx = lax.all_to_all(
        pair_dx.reshape(1, local, groups * cap, width),
        "expert",
        split_axis=2,
        concat_axis=0,
        tiled=True,
    )
    picked_dx = back_dx.reshape(experts * cap, width)[pos].reshape(rows, topk, width)
    grad_tokens = jnp.sum(picked_dx.astype(jnp.float32), axis=1).astype(jnp.bfloat16)
    part_down = jnp.einsum("lrf,lrm->lfm", hidden, dy_in, preferred_element_type=jnp.float32)
    part_gate = jnp.einsum("lrm,lrf->lmf", x_in, grad_a, preferred_element_type=jnp.float32)
    part_up = jnp.einsum("lrm,lrf->lmf", x_in, grad_b, preferred_element_type=jnp.float32)
    summed_gate, summed_up = (
        lax.psum_scatter(
            part_gate.astype(jnp.bfloat16), "dp", scatter_dimension=1, tiled=True
        ).astype(jnp.float32),
        lax.psum_scatter(
            part_up.astype(jnp.bfloat16), "dp", scatter_dimension=1, tiled=True
        ).astype(jnp.float32),
    )
    summed_down = lax.psum_scatter(
        part_down.astype(jnp.bfloat16), "dp", scatter_dimension=2, tiled=True
    )
    return (
        mixed,
        grad_tokens,
        summed_gate.astype(jnp.bfloat16),
        summed_up.astype(jnp.bfloat16),
        summed_down,
    )


def solution(mesh):
    return jax.shard_map(
        per_device,
        mesh=mesh,
        in_specs=(
            P(("expert", "dp"), None),
            P(("expert", "dp"), None),
            P(("expert", "dp"), None),
            P("expert", "dp", None),
            P("expert", "dp", None),
            P("expert", None, "dp"),
            P(("expert", "dp"), None),
        ),
        out_specs=(
            P(("expert", "dp"), None),
            P(("expert", "dp"), None),
            P("expert", "dp", None),
            P("expert", "dp", None),
            P("expert", None, "dp"),
        ),
        check_vma=False,
    )
```

profile of v0, /device:TPU:0, one launch (start us, length us, event | category | flops | bytes accessed | tf_op | source)
XLA Modules:
  0.0 504.0 jit_solution(14802693005822757459)
XLA Ops:
  7.2 0.0 copy-start
  7.2 0.0 all-gather.6.cloned.1.call-start
  7.2 0.7 all-gather.6.cloned.1.call-update
  7.9 0.7 broadcast_multiply_fusion
  8.6 0.8 copy.34
  9.4 0.1 eq.29
  9.5 0.1 eq.25
  9.6 0.1 copy.33
  9.7 0.1 mul.63
  9.8 0.8 copy.32
  10.6 0.1 mul.68
  10.7 0.1 reshape.127
  10.8 18.0 %reduce-window.6 = s32[64,8,128]{2,1,0:T(8,128)S(1)} reduce-window(s32[64,8,128]{2,1,0:T(8,128)S(1)} %fusion.12, s32[]{:T(128)} %constant.6.clone.1), window={size=1x1x128 pad=0_0x0_0x127_0}, to_apply=%region_0.0 | reduce-window | flops 8323072 | bytes 524292 | tf_op jit(solution)/shard_map/reduce-window
  28.8 0.1 slice.16
  29.0 0.1 copy.36
  29.1 0.1 copy.37
  29.2 0.1 broadcast_add_fusion
  29.4 0.1 fusion.11
  29.5 0.0 copy-done
  29.5 24.2 %scatter_custom_fusion.1 = bf16[1536,2048]{1,0:T(8,128)(2,1)} fusion(s32[1024]{0:T(1024)S(1)} %bitcast.83, f32[1024]{0:T(1024)S(1)} %mul.68, bf16[]{:T(256)} %constant.7.clone.1, bf16[128,2048]{1,0:T(8,128)(2,1)S(1)} %copy-done, s32[1024]{0:T(1024)S(1)} %broadcast_clamp_fusion.1), kind=kCustom, calls=%fused_computation.12 | custom fusion | flops 6291456 | bytes 6823938 | tf_op jit(solution)/shard_map/scatter | solution.py:30
  53.7 7.5 %all-to-all-start.2 = ((bf16[32,2,24,2048]{3,2,1,0:T(8,128)(2,1)}), bf16[32,2,24,2048]{3,2,1,0:T(8,128)(2,1)}, u32[]{:S(2)}, u32[]{:S(2)}) async-start(bf16[32,2,24,2048]{3,2,1,0:T(8,128)(2,1)} %bitcast.71), calls=%async_computation.2 | async-start | bytes 12582912 | tf_op jit(solution)/shard_map/all_to_all | solution.py:54
  61.2 0.0 all-gather.4.cloned.1.call-start
  61.3 0.7 all-gather.4.cloned.1.call-update
  62.0 24.4 %scatter_custom_fusion = bf16[1536,2048]{1,0:T(8,128)(2,1)} fusion(s32[1024]{0:T(1024)S(1)} %bitcast.84, bf16[128,2048]{1,0:T(8,128)(2,1)} %param.7, s32[1024]{0:T(1024)S(1)} %broadcast_clamp_fusion.1, bf16[]{:T(256)} %constant.7.clone.1), kind=kCustom, calls=%fused_computation.14 | custom fusion | bytes 6291968 | tf_op jit(solution)/shard_map/scatter | solution.py:25
  86.3 52.8 %all-to-all-done.2 = bf16[32,2,24,2048]{3,2,1,0:T(8,128)(2,1)} async-done(((bf16[32,2,24,2048]{3,2,1,0:T(8,128)(2,1)}), bf16[32,2,24,2048]{3,2,1,0:T(8,128)(2,1)}, u32[]{:S(2)}, u32[]{:S(2)}) %all-to-all-start.2) | async-done | bytes 6291488 | tf_op jit(solution)/shard_map/all_to_all | solution.py:54
  139.1 4.9 all-to-all-start
  144.0 0.0 all-gather.8.cloned.1.call-start
  144.1 0.7 all-gather.8.cloned.1.call-update
  144.7 0.5 reduce-scatter.8.cloned.1.call-start
  145.3 6.6 %copy.42 = bf16[1,2,32,24,2048]{4,3,2,1,0:T(8,128)(2,1)} copy(bf16[1,2,32,24,2048]{4,3,1,2,0:T(8,128)(2,1)} %bitcast.16) | data formatting | bytes 12582912 | tf_op jit(solution)/shard_map/all_to_all | solution.py:54
  151.8 70.1 %all-to-all-done = bf16[32,2,24,2048]{3,2,1,0:T(8,128)(2,1)} async-done(((bf16[32,2,24,2048]{3,2,1,0:T(8,128)(2,1)}), bf16[32,2,24,2048]{3,2,1,0:T(8,128)(2,1)}, u32[]{:S(2)}, u32[]{:S(2)}) %all-to-all-start) | async-done | bytes 6291488 | tf_op jit(solution)/shard_map/all_to_all | solution.py:32
  221.9 6.5 %copy.38 = bf16[1,2,32,24,2048]{4,3,2,1,0:T(8,128)(2,1)} copy(bf16[1,2,32,24,2048]{4,3,1,2,0:T(8,128)(2,1)} %bitcast.7) | data formatting | bytes 12582912 | tf_op jit(solution)/shard_map/all_to_all | solution.py:32
  228.4 8.5 %fusion.15 = f32[2,768,384]{2,1,0:T(8,128)} fusion(bf16[2,768,2048]{2,1,0:T(8,128)(2,1)} %bitcast.72, bf16[2,2048,384]{2,1,0:T(8,128)(2,1)} %all-gather.6.cloned.1.call-done), kind=kOutput, calls=%fused_computation.42 | convolution fusion | flops 2415919104 | bytes 11796480 | tf_op jit(solution)/shard_map/lrm,lmf->lrf/dot_general | solution.py:40
  236.9 8.8 %fusion.14 = f32[2,768,384]{2,1,0:T(8,128)} fusion(bf16[2,768,2048]{2,1,0:T(8,128)(2,1)} %bitcast.73, bf16[2,2048,384]{2,1,0:T(8,128)(2,1)} %all-gather.4.cloned.1.call-done), kind=kOutput, calls=%fused_computation.41 | convolution fusion | flops 2415919104 | bytes 11796480 | tf_op jit(solution)/shard_map/lrm,lmf->lrf/dot_general | solution.py:39
  245.7 10.8 %multiply_convert_fusion.2 = (bf16[2,768,384]{2,1,0:T(8,128)(2,1)}, bf16[2,768,384]{2,1,0:T(8,128)(2,1)}, bf16[2,768,384]{2,1,0:T(8,128)(2,1)S(1)}) fusion(f32[2,768,384]{2,1,0:T(8,128)} %fusion.14, f32[2,768,384]{2,1,0:T(8,128)} %fusion.15, bf16[2,768,2048]{2,1,0:T(8,128)(2,1)} %bitcast.76, bf16[2,384,2048]{2,1,0:T(8,128)(2,1)} %all-gather.8.cloned.1.call-done), kind=kOutput, calls=%fused_computation.22 | convolution fusion | flops 2424766464 | bytes 17694720 | tf_op jit(solution)/shard_map/lrm,lfm->lrf/dot_general | solution.py:56
  256.5 1.0 copy-done.6
  257.5 0.0 slice-done
  257.5 0.0 slice-done.1
  257.5 4.3 convolution_convert_fusion
  261.8 0.0 reduce-scatter.8.cloned.1.call-update
  261.8 5.7 %convert_bitcast_fusion = bf16[1,2,768,2048]{3,2,1,0:T(8,128)(2,1)S(1)} fusion(bf16[2,768,384]{2,1,0:T(8,128)(2,1)} %copy-done.6, bf16[2,384,2048]{2,1,0:T(8,128)(2,1)} %all-gather.8.cloned.1.call-done), kind=kOutput, calls=%fused_computation.11 | convolution fusion | flops 2419064832 | bytes 10616832 | tf_op jit(solution)/shard_map/lrf,lfm->lrm/dot_general | solution.py:42
  267.5 18.8 %copy.39 = bf16[1,2,768,2048]{3,1,0,2:T(2,128)(2,1)} copy(bf16[1,2,768,2048]{3,2,1,0:T(8,128)(2,1)S(1)} %convert_bitcast_fusion) | data formatting | bytes 12582912 | tf_op jit(solution)/shard_map/reshape | solution.py:46
  286.3 5.0 all-to-all-start.1
  291.3 0.0 reduce-scatter.4.cloned.1.call-start
  291.4 8.0 %convolution_convert_fusion.2 = bf16[2,2048,384]{2,1,0:T(8,128)(2,1)} fusion(bf16[2,768,2048]{2,1,0:T(8,128)(2,1)} %bitcast.74, bf16[2,768,384]{2,1,0:T(8,128)(2,1)S(1)} %copy-done.5), kind=kOutput, calls=%fused_computation.19 | convolution fusion | flops 2417491968 | bytes 10616832 | tf_op jit(solution)/shard_map/lrm,lrf->lmf/dot_general | solution.py:73
  299.4 0.0 reduce-scatter.4.cloned.1.call-update
  299.4 0.0 copy-start.3
  299.4 0.0 copy-start.4
  299.4 8.5 %fusion.16 = f32[2,768,2048]{2,1,0:T(8,128)} fusion(bf16[2,768,384]{2,1,0:T(8,128)(2,1)S(1)} %copy-done.5, bf16[2,2048,384]{2,1,0:T(8,128)(2,1)} %all-gather.4.cloned.1.call-done), kind=kOutput, calls=%fused_computation.43 | convolution fusion | flops 2415919104 | bytes 16908288 | tf_op jit(solution)/shard_map/lrf,lmf->lrm/dot_general | solution.py:60
  307.9 0.0 copy-done.4
  307.9 7.1 %fusion.1 = bf16[1,2,768,2048]{3,2,1,0:T(8,128)(2,1)S(1)} fusion(f32[2,768,2048]{2,1,0:T(8,128)} %fusion.16, bf16[2,768,384]{2,1,0:T(8,128)(2,1)S(1)} %copy-done.4, bf16[2,2048,384]{2,1,0:T(8,128)(2,1)S(1)} %copy-done.3), kind=kOutput, calls=%fused_computation.10 | convolution fusion | flops 2422210560 | bytes 23199744 | tf_op jit(solution)/shard_map/lrf,lmf->lrm/dot_general | solution.py:61
  314.9 18.8 %copy.43 = bf16[1,2,768,2048]{3,1,0,2:T(2,128)(2,1)} copy(bf16[1,2,768,2048]{3,2,1,0:T(8,128)(2,1)S(1)} %fusion.1) | data formatting | bytes 12582912 | tf_op jit(solution)/shard_map/reshape | solution.py:64
  333.7 35.5 %all-to-all-done.1 = bf16[1,2,768,2048]{3,1,0,2:T(2,128)(2,1)} async-done(((bf16[1,2,768,2048]{3,1,0,2:T(2,128)(2,1)}), bf16[1,2,768,2048]{3,1,0,2:T(2,128)(2,1)}, u32[]{:S(2)}, u32[]{:S(2)}) %all-to-all-start.1) | async-done | bytes 6291488 | tf_op jit(solution)/shard_map/all_to_all | solution.py:45
  369.2 4.9 all-to-all-start.3
  374.1 0.3 reduce-scatter.6.cloned.1.call-start
  374.4 7.9 %convolution_convert_fusion.1 = bf16[2,2048,384]{2,1,0:T(8,128)(2,1)} fusion(bf16[2,768,2048]{2,1,0:T(8,128)(2,1)} %bitcast.75, bf16[2,768,384]{2,1,0:T(8,128)(2,1)S(1)} %copy-done.4), kind=kOutput, calls=%fused_computation.18 | convolution fusion | flops 2417491968 | bytes 10616832 | tf_op jit(solution)/shard_map/lrm,lrf->lmf/dot_general | solution.py:74
  382.3 0.0 reduce-scatter.6.cloned.1.call-update
  382.3 8.3 %copy.40 = bf16[1,2,32,24,2048]{4,3,1,2,0:T(8,128)(2,1)} copy(bf16[1,2,32,24,2048]{4,1,3,2,0:T(2,128)(2,1)} %bitcast.10) | data formatting | bytes 12582912 | tf_op jit(solution)/shard_map/all_to_all | solution.py:45
  390.6 61.4 %all-to-all-done.3 = bf16[1,2,768,2048]{3,1,0,2:T(2,128)(2,1)} async-done(((bf16[1,2,768,2048]{3,1,0,2:T(2,128)(2,1)}), bf16[1,2,768,2048]{3,1,0,2:T(2,128)(2,1)}, u32[]{:S(2)}, u32[]{:S(2)}) %all-to-all-start.3) | async-done | bytes 6291488 | tf_op jit(solution)/shard_map/all_to_all | solution.py:63
  452.0 8.4 %copy.44 = bf16[1,2,32,24,2048]{4,3,1,2,0:T(8,128)(2,1)} copy(bf16[1,2,32,24,2048]{4,1,3,2,0:T(2,128)(2,1)} %bitcast.19) | data formatting | bytes 12582912 | tf_op jit(solution)/shard_map/all_to_all | solution.py:63
  460.4 12.7 %gather_fusion = bf16[1024,2048]{1,0:T(8,128)(2,1)} fusion(bf16[1536,2048]{1,0:T(8,128)(2,1)} %bitcast.68, s32[1024]{0:T(1024)S(1)} %broadcast_clamp_fusion), kind=kCustom, calls=%fused_computation.1 | custom fusion | bytes 8392704 | tf_op jit(solution)/shard_map/gather | solution.py:52
  473.0 12.5 %gather_fusion.1 = bf16[1024,2048]{1,0:T(8,128)(2,1)} fusion(bf16[1536,2048]{1,0:T(8,128)(2,1)} %bitcast.69, s32[1024]{0:T(1024)S(1)} %broadcast_clamp_fusion), kind=kCustom, calls=%fused_computation.3 | custom fusion | bytes 8392704 | tf_op jit(solution)/shard_map/gather | solution.py:70
  485.5 6.0 %bitcast_reduce_fusion = bf16[128,2048]{1,0:T(8,128)(2,1)} fusion(bf16[1024,2048]{1,0:T(8,128)(2,1)} %gather_fusion.1), kind=kLoop, calls=%fused_computation.13 | loop fusion | flops 1835008 | bytes 4718592 | tf_op jit(solution)/shard_map/reduce_sum | solution.py:71
  491.5 5.2 %fusion = bf16[128,2048]{1,0:T(8,128)(2,1)} fusion(bf16[1024,2048]{1,0:T(8,128)(2,1)S(1)} %copy-done.2, f32[128,8]{1,0:T(8,128)S(1)} %copy.32), kind=kLoop, calls=%fused_computation.8 | loop fusion | flops 6029312 | bytes 4722688 | tf_op jit(solution)/shard_map/reduce_sum | solution.py:53
  (25 shorter events, 0.1 us)
Async XLA Ops:
  7.2 22.3 %copy-start = (bf16[128,2048]{1,0:T(8,128)(2,1)S(1)}, bf16[128,2048]{1,0:T(8,128)(2,1)}, u32[]{:S(2)}) copy-start(bf16[128,2048]{1,0:T(8,128)(2,1)} %param.13) | copy-start | bytes 1572868
  7.2 221.2 %all-gather.6.cloned.1.call-start = ((), (), s32[]{:S(2)}) async-start(), calls=%async_computation.8 | async-start | bytes 3932160 | tf_op jit(solution)/shard_map/all_gather | solution.py:36
  53.7 85.4 %all-to-all-start.2 = ((bf16[32,2,24,2048]{3,2,1,0:T(8,128)(2,1)}), bf16[32,2,24,2048]{3,2,1,0:T(8,128)(2,1)}, u32[]{:S(2)}, u32[]{:S(2)}) async-start(bf16[32,2,24,2048]{3,2,1,0:T(8,128)(2,1)} %bitcast.71), calls=%async_computation.2 | async-start | bytes 12582912 | tf_op jit(solution)/shard_map/all_to_all | solution.py:54
  61.2 175.7 %all-gather.4.cloned.1.call-start = ((), (), s32[]{:S(2)}) async-start(), calls=%async_computation.7 | async-start | bytes 3932160 | tf_op jit(solution)/shard_map/all_gather | solution.py:35
  139.1 82.8 %all-to-all-start = ((bf16[32,2,24,2048]{3,2,1,0:T(8,128)(2,1)}), bf16[32,2,24,2048]{3,2,1,0:T(8,128)(2,1)}, u32[]{:S(2)}, u32[]{:S(2)}) async-start(bf16[32,2,24,2048]{3,2,1,0:T(8,128)(2,1)} %bitcast.70), calls=%async_computation | async-start | bytes 12582912 | tf_op jit(solution)/shard_map/all_to_all | solution.py:32
  144.0 101.7 %all-gather.8.cloned.1.call-start = ((), (), s32[]{:S(2)}) async-start(), calls=%async_computation.9 | async-start | bytes 3932160 | tf_op jit(solution)/shard_map/all_gather | solution.py:38
  144.7 352.0 %reduce-scatter.8.cloned.1.call-start = ((), (), s32[]{:S(2)}) async-start(), calls=%async_computation.12 | async-start | bytes 3932160 | tf_op jit(solution)/shard_map/reduce_scatter | solution.py:83
  236.9 20.6 %slice-start = ((s8[6291456]{0:T(1024)(128)(4,1)}), s8[2097152]{0:T(1024)(128)(4,1)S(1)}, s32[]{:S(2)}) async-start(s8[6291456]{0:T(1024)(128)(4,1)} %bitcast.77), calls=%async_computation.13 | async-start | bytes 4194304
  245.7 11.8 %slice-start.1 = ((s8[6291456]{0:T(1024)(128)(4,1)}), s8[4194304]{0:T(1024)(128)(4,1)S(1)}, s32[]{:S(2)}) async-start(s8[6291456]{0:T(1024)(128)(4,1)} %bitcast.77), calls=%async_computation.14 | async-start | bytes 8388608
  256.5 1.0 copy-start.6
  286.3 5.1 %copy-start.5 = (bf16[2,768,384]{2,1,0:T(8,128)(2,1)S(1)}, bf16[2,768,384]{2,1,0:T(8,128)(2,1)}, u32[]{:S(2)}) copy-start(bf16[2,768,384]{2,1,0:T(8,128)(2,1)} %get-tuple-element.6) | copy-start | bytes 3538948
  286.3 82.9 %all-to-all-start.1 = ((bf16[1,2,768,2048]{3,1,0,2:T(2,128)(2,1)}), bf16[1,2,768,2048]{3,1,0,2:T(2,128)(2,1)}, u32[]{:S(2)}, u32[]{:S(2)}) async-start(bf16[1,2,768,2048]{3,1,0,2:T(2,128)(2,1)} %copy.39), calls=%async_computation.1 | async-start | bytes 12582912 | tf_op jit(solution)/shard_map/all_to_all | solution.py:45
  291.3 205.4 %reduce-scatter.4.cloned.1.call-start = ((), (), s32[]{:S(2)}) async-start(), calls=%async_computation.10 | async-start | bytes 3932160 | tf_op jit(solution)/shard_map/reduce_scatter | solution.py:76
  299.4 8.5 %copy-start.3 = (bf16[2,2048,384]{2,1,0:T(8,128)(2,1)S(1)}, bf16[2,2048,384]{2,1,0:T(8,128)(2,1)}, u32[]{:S(2)}) copy-start(bf16[2,2048,384]{2,1,0:T(8,128)(2,1)} %all-gather.6.cloned.1.call-done) | copy-start | bytes 9437188
  299.4 8.5 %copy-start.4 = (bf16[2,768,384]{2,1,0:T(8,128)(2,1)S(1)}, bf16[2,768,384]{2,1,0:T(8,128)(2,1)}, u32[]{:S(2)}) copy-start(bf16[2,768,384]{2,1,0:T(8,128)(2,1)} %get-tuple-element.5) | copy-start | bytes 3538948
  369.2 82.8 %all-to-all-start.3 = ((bf16[1,2,768,2048]{3,1,0,2:T(2,128)(2,1)}), bf16[1,2,768,2048]{3,1,0,2:T(2,128)(2,1)}, u32[]{:S(2)}, u32[]{:S(2)}) async-start(bf16[1,2,768,2048]{3,1,0,2:T(2,128)(2,1)} %copy.43), calls=%async_computation.3 | async-start | bytes 12582912 | tf_op jit(solution)/shard_map/all_to_all | solution.py:63
  374.1 122.6 %reduce-scatter.6.cloned.1.call-start = ((), (), s32[]{:S(2)}) async-start(), calls=%async_computation.11 | async-start | bytes 3932160 | tf_op jit(solution)/shard_map/reduce_scatter | solution.py:79
  473.0 23.7 %copy-start.1 = (bf16[128,2048]{1,0:T(8,128)(2,1)S(1)}, bf16[128,2048]{1,0:T(8,128)(2,1)}, u32[]{:S(2)}) copy-start(bf16[128,2048]{1,0:T(8,128)(2,1)} %param.13) | copy-start | bytes 1572868
  485.5 6.0 %copy-start.2 = (bf16[1024,2048]{1,0:T(8,128)(2,1)S(1)}, bf16[1024,2048]{1,0:T(8,128)(2,1)}, u32[]{:S(2)}) copy-start(bf16[1024,2048]{1,0:T(8,128)(2,1)} %gather_fusion) | copy-start | bytes 12582916
Sparse Core Ops, SparseCore 0:
  9.7 42.2 all-gather.5
  63.7 42.1 all-gather.3
  146.5 42.1 all-gather.7
  261.9 36.2 reduce-scatter.7
  301.0 39.3 reduce-scatter.3
  382.4 40.8 reduce-scatter.5
where the time goes:
time: 513 us; the launch traced here: 504 us
  waiting for transfers between devices  222 us (43%)
  local copies, waits for them, and re-layouts  120 us (23%)
  matrix products  69.4 us (14%)
  other arithmetic  54.4 us (11%)
  starting transfers between devices  23.3 us (5%)
  between operations  14.7 us (3%)
    all_to_all x1, waiting for transfers between devices, per_device(): lax.all_to_all(send_x, 'expert', split_axis=0, concat_axis=2, tiled=True)  70.1 us
    all_to_all x1, waiting for transfers between devices, per_device(): lax.all_to_all(pair_dx.reshape(1, local, groups * cap, width), 'expert',...  61.4 us
    all_to_all x1, waiting for transfers between devices, per_device(): lax.all_to_all(send_g, 'expert', split_axis=0, concat_axis=2, tiled=True)  52.8 us
    all_to_all x1, waiting for transfers between devices, per_device(): lax.all_to_all(expert_out.reshape(1, local, groups * cap, width), 'expert...  35.5 us
    scatter x1, local copies, waits for them, and re-layouts, per_device(): jnp.zeros((experts * cap, width), jnp.bfloat16).at[pos]  24.4 us
    scatter x1, other arithmetic, per_device(): jnp.zeros((experts * cap, width), jnp.bfloat16).at[pos].set(pair_grad)  24.2 us
    reshape x1, local copies, waits for them, and re-layouts, per_device(): pair_dx.reshape(1, local, groups * cap, width)  18.8 us
    reshape x1, local copies, waits for them, and re-layouts, per_device(): expert_out.reshape(1, local, groups * cap, width)  18.8 us
  transfers between devices with their start and end apart: 10, of which 4 were waited for; matrix products, arithmetic and copies ran while one was open for 45% of the time, Pallas kernels for 0%

commit v1 on v0

v1 whole, which is shorter than its diff:
```python
import jax
import jax.numpy as jnp
from jax import lax
from jax.experimental import pallas as pl
from jax.experimental.pallas import tpu as pltpu
from jax.sharding import PartitionSpec as P

MESH = pl.DeviceIdType.MESH
BF = jnp.bfloat16
F32 = jnp.float32
D = 2048
FF = 384
TOK = 128
CAP = 24
ROWS = 768
XW = D + 128
NT = (((1,), (1,)), ((), ()))
TN = (((0,), (0,)), ((), ()))
NN = (((1,), (0,)), ((), ()))


def dot(a, b, dims):
    return lax.dot_general(a, b, dims, preferred_element_type=F32)


def kernel(
    xm, g, wgate, wup, wdown,
    mixed, gtok, ggate, gup, gdown,
    xbuf, gbuf, ysib, qopp, qfull, popp, pfull,
    S, L, Wgu, Wd, YD, H, DAB, PW, P4, MB, YL, RB, zhg, zfg, zhd, zfd,
    a_send, a_recv, s_send, s_recv, w_send, w_recv, y_send, y_recv,
    q_send, q_recv, p_send, p_recv, z_send, z_recv, loc, ld, yl_sem,
):
    me = lax.axis_index("expert")
    z = lax.axis_index("dp")
    c = lax.rem(me, 2)
    x = lax.rem(me // 2, 4)
    y = me // 8
    sib = {"expert": me + 1 - 2 * c}
    zr, zl, zo = lax.rem(z + 1, 4), lax.rem(z + 3, 4), lax.rem(z + 2, 4)

    def pq(dp, dq):
        dx = dp + c * (dq - dp)
        dy = dq + c * (dp - dq)
        return {"expert": (lax.rem(y + dy, 4) * 4 + lax.rem(x + dx, 4)) * 2 + c}

    dev = {"P+": pq(1, 0), "P-": pq(3, 0), "Q+": pq(0, 1), "Q-": pq(0, 3), "S": sib, "Z+": {"dp": zr}, "Z-": {"dp": zl}}

    def slot(dp, dq):
        k0, k1 = dp * 4 + dq, dq * 4 + dp
        return k0 + c * (k1 - k0)

    barrier = pltpu.get_barrier_semaphore()
    for d in dev.values():
        pl.semaphore_signal(barrier, inc=1, device_id=d, device_id_type=MESH)
    pl.semaphore_wait(barrier, 7)

    pending = []

    def send(src, dst, ssem, rsem, to):
        cp = pltpu.make_async_remote_copy(
            src_ref=src, dst_ref=dst, send_sem=ssem, recv_sem=rsem, device_id=dev[to], device_id_type=MESH
        )
        cp.start()
        pending.append(cp)

    def arrived(dst, ssem, rsem):
        pltpu.make_async_remote_copy(
            src_ref=dst, dst_ref=dst, send_sem=ssem, recv_sem=rsem, device_id=dev["S"], device_id_type=MESH
        ).wait_recv()

    half = pl.ds(pl.multiple_of(c * TOK, TOK), TOK)
    other = pl.ds(pl.multiple_of((1 - c) * TOK, TOK), TOK)
    bufs = (xbuf, gbuf)
    counts = {"a": 0, "q": 0, "p": 0, "z": 0, "w": 0}

    def nxt(name):
        counts[name] += 1
        return counts[name] - 1

    def aidx(dp, dq, k):
        return (dp * 4 + dq) * 2 + k

    def blk(dp, dq, k):
        if dp == 0 and dq == 0:
            return (xm, g)[k]
        return bufs[k].at[slot(dp, dq), half, :]

    def push(dp, dq, k, to):
        ddp, ddq = dp, dq
        if to == "P+":
            ddp = (dp + 3) % 4
        elif to == "P-":
            ddp = (dp + 1) % 4
        elif to == "Q+":
            ddq = (dq + 3) % 4
        elif to == "Q-":
            ddq = (dq + 1) % 4
        send(blk(dp, dq, k), bufs[k].at[slot(ddp, ddq), half, :], a_send.at[nxt("a")], a_recv.at[aidx(ddp, ddq, k)], to)

    def push_sib(dp, dq, k):
        i = aidx(dp, dq, k)
        send(blk(dp, dq, k), bufs[k].at[slot(dp, dq), half, :], s_send.at[i], s_recv.at[i], "S")

    def take(dp, dq, k):
        i = aidx(dp, dq, k)
        arrived(bufs[k].at[slot(dp, dq), half, :], a_send.at[0], a_recv.at[i])

    def take_sib(dp, dq, k):
        i = aidx(dq, dp, k)
        arrived(bufs[k].at[slot(dp, dq), other, :], s_send.at[0], s_recv.at[i])

    for to in ("P+", "P-", "Q+", "Q-"):
        push(0, 0, 0, to)
    for to in ("P+", "P-", "Q+", "Q-"):
        push(0, 0, 1, to)

    def zrows(i):
        return pl.ds(pl.multiple_of(i * 512, 512), 512)

    wsrc = (wgate, wup, wdown)

    def wdst(k, i):
        if k == 2:
            return Wd.at[:, i]
        return Wgu.at[:, zrows(i), pl.ds(k * FF, FF)]

    for k in range(3):
        send(wsrc[k], wdst(k, z), w_send.at[nxt("w")], w_recv.at[k], "Z+")
        send(wsrc[k], wdst(k, z), w_send.at[nxt("w")], w_recv.at[3 + k], "Z-")
    own = [
        pltpu.make_async_copy(xm, xbuf.at[0, half, :], loc.at[0]),
        pltpu.make_async_copy(g, gbuf.at[0, half, :], loc.at[1]),
    ] + [pltpu.make_async_copy(wsrc[k], wdst(k, z), loc.at[2 + k]) for k in range(3)]
    for cp in own:
        cp.start()
    push_sib(0, 0, 0)
    push_sib(0, 0, 1)

    def w_fwd_gu():
        for k in (0, 1):
            arrived(wdst(k, zl), w_send.at[0], w_recv.at[k])
            arrived(wdst(k, zr), w_send.at[0], w_recv.at[3 + k])
        send(Wgu.at[0, zrows(zl)], Wgu.at[0, zrows(zl)], w_send.at[nxt("w")], w_recv.at[6], "Z+")
        send(Wgu.at[1, zrows(zr)], Wgu.at[1, zrows(zr)], w_send.at[nxt("w")], w_recv.at[7], "Z-")

    def w_fwd_d():
        arrived(wdst(2, zl), w_send.at[0], w_recv.at[2])
        arrived(wdst(2, zr), w_send.at[0], w_recv.at[5])
        send(Wd.at[0, zl], Wd.at[0, zl], w_send.at[nxt("w")], w_recv.at[8], "Z+")
        send(Wd.at[1, zr], Wd.at[1, zr], w_send.at[nxt("w")], w_recv.at[9], "Z-")

    def w_last():
        arrived(Wgu.at[0, zrows(zo)], w_send.at[0], w_recv.at[6])
        arrived(Wgu.at[1, zrows(zo)], w_send.at[0], w_recv.at[7])
        arrived(Wd.at[0, zo], w_send.at[0], w_recv.at[8])
        arrived(Wd.at[1, zo], w_send.at[0], w_recv.at[9])

    tri = (
        lax.broadcasted_iota(jnp.int32, (TOK, TOK), 0) <= lax.broadcasted_iota(jnp.int32, (TOK, TOK), 1)
    ).astype(F32).astype(BF)
    row8 = lax.broadcasted_iota(jnp.int32, (8, TOK), 0)
    slot_row = lax.broadcasted_iota(jnp.int32, (2 * CAP, TOK), 0).astype(F32)
    cf = c.astype(F32)
    e_own = (2 * me).astype(F32)
    e_sib = (2 * (me + 1 - 2 * c)).astype(F32)

    def load(chip, b):
        r = slot(*chip)
        for cp in load_copies(r, b):
            cp.start()

    def load_copies(r, b):
        return (
            pltpu.make_async_copy(xbuf.at[r, :, pl.ds(0, D)], L.at[pl.ds(b * 512, 256), :], ld.at[b, 0]),
            pltpu.make_async_copy(gbuf.at[r], L.at[pl.ds(b * 512 + 256, 256), :], ld.at[b, 1]),
            pltpu.make_async_copy(xbuf.at[r, pl.ds(0, 32), pl.ds(D, 128)], MB.at[b, 0], ld.at[b, 2]),
            pltpu.make_async_copy(xbuf.at[r, pl.ds(TOK, 32), pl.ds(D, 128)], MB.at[b, 1], ld.at[b, 3]),
        )

    def pick(chip, b):
        r = slot(*chip)
        for cp in load_copies(r, b):
            cp.wait()
        ids, prob = [], []
        for t in range(2):
            ids.append(MB[b, t, 0:8].astype(F32))
            prob.append(
                MB[b, t, 8:16].astype(F32) + (MB[b, t, 16:24].astype(F32) + MB[b, t, 24:32].astype(F32))
            )
        ids_c = jnp.where(c == 0, ids[0], ids[1])
        todo = [(ids[0], e_own), (ids[1], e_own), (ids[0], e_own + 1), (ids[1], e_own + 1), (ids_c, e_sib), (ids_c, e_sib + 1)]
        hit = jnp.zeros((8, TOK), F32)
        pv = []
        for j, (idv, e) in enumerate(todo):
            m = jnp.where(idv == e, 1.0, 0.0)
            if j < 4:
                pv.append(jnp.sum(m * prob[j % 2], axis=0, keepdims=True))
            hit = jnp.where(row8 == j, jnp.sum(m, axis=0, keepdims=True), hit)
        rank = dot(hit.astype(BF), tri, NN)
        key = jnp.where(hit > 0.5, rank - 1.0, -1000.0)
        p256, pown, psib = [], [], []
        for e in range(2):
            p0 = jnp.where(key[2 * e : 2 * e + 1] == slot_row, 1.0, 0.0)
            p1 = jnp.where(key[2 * e + 1 : 2 * e + 2] + CAP == slot_row, 1.0, 0.0)
            w = jnp.sum(p0 * pv[2 * e] + p1 * pv[2 * e + 1], axis=1, keepdims=True)
            at = pl.ds(pl.multiple_of(e * ROWS + r * 48, 16), 48)
            PW[at, :] = jnp.broadcast_to(w, (48, 128))
            p256.append(jnp.concatenate([p0, p1], axis=1))
            pown.append(jnp.where(c == 0, p0, p1))
            psib.append(jnp.where(key[4 + e : 5 + e] + CAP * cf == slot_row, 1.0, 0.0))
        P4[r] = jnp.concatenate(pown + psib, axis=0).astype(BF)
        pick_m = jnp.concatenate(p256, axis=0).astype(BF)

        def cols(n, _):
            cc = pl.ds(pl.multiple_of(n * 1024, 1024), 1024)
            for t in range(2):
                src = L[pl.ds(b * 512 + t * 256, 256), cc]
                got = dot(pick_m, src, NN).astype(BF)
                for e in range(2):
                    at = pl.ds(pl.multiple_of(t * 2 * ROWS + e * ROWS + r * 48, 16), 48)
                    S[at, cc] = got[e * 48 : e * 48 + 48]
            return 0

        lax.fori_loop(0, 2, cols, 0)

    def picks(chips):
        for i, chip in enumerate(chips):
            if i == 0:
                for k in range(2):
                    if chip != (0, 0) or k >= 0:
                        take_sib(chip[0], chip[1], k)
                load(chip, 0)
            if i + 1 < len(chips):
                for k in range(2):
                    take_sib(chips[i + 1][0], chips[i + 1][1], k)
                load(chips[i + 1], (i + 1) % 2)
            pick(chip, i % 2)

    take(3, 0, 0)
    push(3, 0, 0, "P+")
    push(3, 0, 0, "Q+")
    push(3, 0, 0, "Q-")
    take(1, 0, 0)
    push(1, 0, 0, "Q+")
    push(1, 0, 0, "Q-")
    take(1, 0, 1)
    push(1, 0, 1, "P-")
    push(1, 0, 1, "Q+")
    push(1, 0, 1, "Q-")
    take(3, 0, 1)
    push(3, 0, 1, "Q+")
    push(3, 0, 1, "Q-")

    def second_ring(dp):
        take(dp, 3, 0)
        push(dp, 3, 0, "Q+")
        take(dp, 1, 1)
        push(dp, 1, 1, "Q-")
        take(dp, 1, 0)
        take(dp, 3, 1)
        for dq in (3, 1):
            push_sib(dp, dq, 0)
            push_sib(dp, dq, 1)

    second_ring(0)
    for dp in (3, 1):
        push_sib(dp, 0, 0)
        push_sib(dp, 0, 1)
    for cp in own:
        cp.wait()
    picks([(0, 0)])
    w_fwd_gu()
    take(2, 0, 0)
    push(2, 0, 0, "Q+")
    push(2, 0, 0, "Q-")
    take(2, 0, 1)
    push(2, 0, 1, "Q+")
    push(2, 0, 1, "Q-")
    push_sib(2, 0, 0)
    push_sib(2, 0, 1)
    picks([(0, 3), (0, 1), (3, 0), (1, 0)])
    second_ring(3)
    second_ring(1)
    for k in range(2):
        take(0, 2, k)
        push_sib(0, 2, k)
    w_fwd_d()
    picks([(2, 0), (0, 2), (3, 3), (3, 1), (1, 3), (1, 1)])
    second_ring(2)
    for dp in (3, 1, 2):
        for k in range(2):
            take(dp, 2, k)
            push_sib(dp, 2, k)
    picks([(2, 3), (2, 1), (3, 2), (1, 2), (2, 2)])
    w_last()

    def forward(e):
        def tile(m, _):
            at = pl.ds(pl.multiple_of(m * 384, 384), 384)
            xs = S[pl.ds(pl.multiple_of(e * ROWS + m * 384, 384), 384), :]
            ab = dot(xs, Wgu[e], NN)
            gs_at = pl.ds(pl.multiple_of((2 + e) * ROWS + m * 384, 384), 384)
            dh = dot(S[gs_at, 0:512], Wd[e, 0], NT)
            for i in range(1, 4):
                dh = dh + dot(S[gs_at, i * 512 : i * 512 + 512], Wd[e, i], NT)
            w = PW[pl.ds(pl.multiple_of(e * ROWS + m * 384, 384), 384), 0:1]
            a, b = ab[:, :FF], ab[:, FF:]
            s = 1.0 / (1.0 + jnp.exp(-a))
            act = a * s
            dh = dh * w
            H[at, :] = (act * b * w).astype(BF)
            DAB[at, 0:FF] = (dh * b * s * (1.0 + a * (1.0 - s))).astype(BF)
            DAB[at, FF:] = (dh * act).astype(BF)
            return 0

        lax.fori_loop(0, 2, tile, 0)

    def outputs(e):
        def tile(m, _):
            at = pl.ds(pl.multiple_of(m * 384, 384), 384)
            for i in range(4):
                yv = dot(H[at, :], Wd[e, i], NN).astype(BF)
                YD[pl.ds(m * 8, 8), e * 48 : e * 48 + 48, i * 512 : i * 512 + 512] = yv.reshape(8, 48, 512)
            for i in range(4):
                dv = dot(DAB[at, :], Wgu[e, i * 512 : i * 512 + 512, :], NT).astype(BF)
                YD[pl.ds(m * 8, 8), e * 48 : e * 48 + 48, D + i * 512 : D + i * 512 + 512] = dv.reshape(8, 48, 512)
            return 0

        lax.fori_loop(0, 2, tile, 0)

    def weight_grads(e):
        def part(i, _):
            cc = zrows(i)
            xs = S[e * ROWS : e * ROWS + ROWS, cc]
            gs = S[(2 + e) * ROWS : (3 + e) * ROWS, cc]
            Wgu[e, cc, :] = dot(xs, DAB[...], TN).astype(BF)
            Wd[e, i] = dot(H[...], gs, TN).astype(BF)
            return 0

        lax.fori_loop(0, 4, part, 0)

    def zblk(e, i):
        return pl.ds(pl.multiple_of(i * 512, 512), 512)

    def zsend(src, dst, i, to):
        send(src, dst, z_send.at[i], z_recv.at[i], to)

    def z_first(e):
        base = e * 8
        lo = pl.ds(pl.multiple_of(zo * 512, 512), 256)
        hi = pl.ds(pl.multiple_of(zo * 512 + 256, 256), 256)
        zsend(Wgu.at[e, lo], zhg.at[e, 0], base + 0, "Z+")
        zsend(Wgu.at[e, hi], zhg.at[e, 1], base + 1, "Z-")
        zsend(Wd.at[e, zo, pl.ds(0, 192)], zhd.at[e, 0], base + 2, "Z+")
        zsend(Wd.at[e, zo, pl.ds(192, 192)], zhd.at[e, 1], base + 3, "Z-")

    def z_second(e):
        base = e * 8
        for i, (dst, rows) in enumerate(((zhg.at[e, 0], 0), (zhg.at[e, 1], 0), (zhd.at[e, 0], 0), (zhd.at[e, 1], 0))):
            arrived(dst, z_send.at[0], z_recv.at[base + i])

        def add(j, _):
            for i, (zz, off) in enumerate(((zr, 0), (zl, 256))):
                at = pl.ds(pl.multiple_of(zz * 512 + off + j * 32, 32), 32)
                Wgu[e, at, :] = (Wgu[e, at, :].astype(F32) + zhg[e, i, pl.ds(j * 32, 32), :].astype(F32)).astype(BF)
            return 0

        lax.fori_loop(0, 8, add, 0)

        def add_d(j, _):
            for i, (zz, off) in enumerate(((zr, 0), (zl, 192))):
                at = pl.ds(pl.multiple_of(off + j * 32, 32), 32)
                Wd[e, zz, at, :] = (Wd[e, zz, at, :].astype(F32) + zhd[e, i, pl.ds(j * 32, 32), :].astype(F32)).astype(BF)
            return 0

        lax.fori_loop(0, 6, add_d, 0)
        zsend(Wgu.at[e, zrows(zr)], zfg.at[e, 0], base + 4, "Z+")
        zsend(Wgu.at[e, zrows(zl)], zfg.at[e, 1], base + 5, "Z-")
        zsend(Wd.at[e, zr], zfd.at[e, 0], base + 6, "Z+")
        zsend(Wd.at[e, zl], zfd.at[e, 1], base + 7, "Z-")

    outs = []

    def z_third(e):
        base = e * 8
        for i, dst in enumerate((zfg.at[e, 0], zfg.at[e, 1], zfd.at[e, 0], zfd.at[e, 1])):
            arrived(dst, z_send.at[0], z_recv.at[base + 4 + i])

        def add(j, _):
            at = pl.ds(pl.multiple_of(z * 512 + j * 32, 32), 32)
            jj = pl.ds(pl.multiple_of(j * 32, 32), 32)
            Wgu[e, at, :] = (
                Wgu[e, at, :].astype(F32) + zfg[e, 0, jj, :].astype(F32) + zfg[e, 1, jj, :].astype(F32)
            ).astype(BF)
            return 0

        lax.fori_loop(0, 16, add, 0)

        def add_d(j, _):
            jj = pl.ds(pl.multiple_of(j * 32, 32), 32)
            Wd[e, z, jj, :] = (
                Wd[e, z, jj, :].astype(F32) + zfd[e, 0, jj, :].astype(F32) + zfd[e, 1, jj, :].astype(F32)
            ).astype(BF)
            return 0

        lax.fori_loop(0, 12, add_d, 0)
        for i, cp in enumerate(
            (
                (Wgu.at[e, zrows(z), pl.ds(0, FF)], ggate.at[e]),
                (Wgu.at[e, zrows(z), pl.ds(FF, FF)], gup.at[e]),
                (Wd.at[e, z], gdown.at[e]),
            )
        ):
            cp = pltpu.make_async_copy(cp[0], cp[1], loc.at[5 + e * 3 + i])
            cp.start()
            outs.append(cp)

    groups = (2, 1, 3, 0)
    order = (2, 1, 3, 0)
    chips = [(dp, dq) for dp in groups for dq in order]

    def yd_sends():
        for i, (dp, dq) in enumerate(chips):
            r = slot(dq, dp)
            send(YD.at[r], ysib.at[r], y_send.at[i], y_recv.at[i], "S")

    def yd_load(i):
        r = slot(*chips[i])
        return pltpu.make_async_copy(ysib.at[r], YL.at[i % 2], yl_sem.at[i % 2])

    def yd_start(i):
        r = slot(*chips[i])
        arrived(ysib.at[r], y_send.at[0], y_recv.at[i])
        yd_load(i).start()

    def cblk(gi, dq, k=0, n=1):
        row = dq * 256 + k * 128
        if gi == 0:
            return L, row, n * 128
        return S, (gi - 1) * 1024 + row, n * 128

    def cref(gi, dq, k=0, n=1):
        ref, row, cnt = cblk(gi, dq, k, n)
        return ref.at[pl.ds(row, cnt), :]

    def combine(gi):
        for j, dq in enumerate(order):
            i = gi * 4 + j
            if i == 0:
                yd_start(0)
            if i + 1 < 16:
                yd_start(i + 1)
            yd_load(i).wait()
            r = slot(*chips[i])
            ref, row, _ = cblk(gi, dq)
            pm = P4[r]

            def cols(n, _):
                cc = pl.ds(pl.multiple_of(n * 512, 512), 512)
                for k in range(2):
                    ck = pl.ds(pl.multiple_of(k * D + n * 512, 512), 512)
                    rows = jnp.concatenate([YD[r, :, ck], YL[i % 2, :, ck]], axis=0)
                    ref[row + k * 128 : row + k * 128 + 128, cc] = dot(pm, rows, TN).astype(BF)
                return 0

            lax.fori_loop(0, 4, cols, 0)

    def fetch(pairs):
        cps = [pltpu.make_async_copy(s, d, ld.at[0, i]) for i, (s, d) in enumerate(pairs)]
        for cp in cps:
            cp.start()
        for cp in cps:
            cp.wait()

    def accumulate(gi, dq, k, n, parts):
        ref, row, cnt = cblk(gi, dq, k, n)

        def add(j, _):
            at = pl.ds(pl.multiple_of(row + j * 16, 16), 16)
            total = ref[at, :].astype(F32)
            for off in parts:
                total = total + RB[pl.ds(pl.multiple_of(off + j * 16, 16), 16), :].astype(F32)
            ref[at, :] = total.astype(BF)
            return 0

        lax.fori_loop(0, cnt // 16, add, 0)

    def qsend(src, dst, gi, j, to):
        send(src, dst, q_send.at[gi * 4 + j], q_recv.at[gi * 4 + j], to)

    def q_first(gi):
        qsend(cref(gi, 2, 0), qopp.at[gi, 0], gi, 0, "Q+")
        qsend(cref(gi, 2, 1), qopp.at[gi, 1], gi, 1, "Q-")

    def q_second(gi):
        arrived(qopp.at[gi, 0], q_send.at[0], q_recv.at[gi * 4 + 0])
        arrived(qopp.at[gi, 1], q_send.at[0], q_recv.at[gi * 4 + 1])
        fetch([(qopp.at[gi, 0], RB.at[pl.ds(512, 128)]), (qopp.at[gi, 1], RB.at[pl.ds(640, 128)])])
        accumulate(gi, 1, 0, 1, (512,))
        qsend(cref(gi, 1, 0, 2), qfull.at[gi, 0], gi, 2, "Q+")
        accumulate(gi, 3, 1, 1, (640,))
        qsend(cref(gi, 3, 0, 2), qfull.at[gi, 1], gi, 3, "Q-")

    def psend(src, dst, j, to):
        send(src, dst, p_send.at[j], p_recv.at[j], to)

    def q_third(gi):
        arrived(qfull.at[gi, 0], q_send.at[0], q_recv.at[gi * 4 + 2])
        arrived(qfull.at[gi, 1], q_send.at[0], q_recv.at[gi * 4 + 3])
        fetch([(qfull.at[gi, 0], RB.at[pl.ds(0, 256)]), (qfull.at[gi, 1], RB.at[pl.ds(256, 256)])])
        accumulate(gi, 0, 0, 2, (0, 256))
        if gi == 0:
            psend(cref(0, 0, 0), popp.at[0], 0, "P+")
            psend(cref(0, 0, 1), popp.at[1], 1, "P-")
        elif gi == 1:
            arrived(popp.at[0], p_send.at[0], p_recv.at[0])
            fetch([(popp.at[0], RB.at[pl.ds(512, 128)])])
            accumulate(1, 0, 0, 1, (512,))
            psend(cref(1, 0, 0, 2), pfull.at[0], 2, "P+")
        elif gi == 2:
            arrived(popp.at[1], p_send.at[0], p_recv.at[1])
            fetch([(popp.at[1], RB.at[pl.ds(512, 128)])])
            accumulate(2, 0, 1, 1, (512,))
            psend(cref(2, 0, 0, 2), pfull.at[1], 3, "P-")
        else:
            arrived(pfull.at[0], p_send.at[0], p_recv.at[2])
            arrived(pfull.at[1], p_send.at[0], p_recv.at[3])
            fetch([(pfull.at[0], RB.at[pl.ds(0, 256)]), (pfull.at[1], RB.at[pl.ds(256, 256)])])
            accumulate(3, 0, 0, 2, (0, 256))
            for k, out in enumerate((mixed, gtok)):
                cp = pltpu.make_async_copy(cref(3, 0, k), out, loc.at[11 + k])
                cp.start()
                outs.append(cp)

    def end_sends():
        for cp in pending:
            cp.wait_send()
        pending.clear()

    forward(0)
    outputs(0)
    end_sends()
    weight_grads(0)
    z_first(0)
    forward(1)
    outputs(1)
    yd_sends()
    weight_grads(1)
    z_first(1)
    z_second(0)
    combine(0)
    q_first(0)
    combine(1)
    q_first(1)
    q_second(0)
    z_second(1)
    combine(2)
    q_first(2)
    q_second(1)
    q_third(0)
    combine(3)
    q_first(3)
    q_second(2)
    q_third(1)
    z_third(0)
    q_second(3)
    q_third(2)
    z_third(1)
    q_third(3)
    for cp in outs:
        cp.wait()
    end_sends()


def per_device(tokens, expert_ids, gate_prob, w_gate, w_up, w_down, grad_out):
    ids = expert_ids.T.astype(BF)
    p = gate_prob.T
    hi = lax.reduce_precision(p, 8, 7)
    rest = p - hi
    mid = lax.reduce_precision(rest, 8, 7)
    low = rest - mid
    meta = jnp.concatenate(
        [ids, hi.astype(BF), mid.astype(BF), low.astype(BF), jnp.zeros((96, TOK), BF)], axis=0
    )
    xm = jnp.concatenate([tokens, meta], axis=1)
    sds = jax.ShapeDtypeStruct
    hbm = pl.BlockSpec(memory_space=pl.ANY)
    dma = pltpu.SemaphoreType.DMA
    out_shape = (
        sds((TOK, D), BF),
        sds((TOK, D), BF),
        sds((2, 512, FF), BF),
        sds((2, 512, FF), BF),
        sds((2, FF, 512), BF),
        sds((16, 256, XW), BF),
        sds((16, 256, D), BF),
        sds((16, 96, 2 * D), BF),
        sds((4, 2, TOK, D), BF),
        sds((4, 2, 256, D), BF),
        sds((2, TOK, D), BF),
        sds((2, 256, D), BF),
    )
    scratch = [
        pltpu.VMEM((4 * ROWS, D), BF),
        pltpu.VMEM((1024, D), BF),
        pltpu.VMEM((2, D, 2 * FF), BF),
        pltpu.VMEM((2, 4, FF, 512), BF),
        pltpu.VMEM((16, 96, 2 * D), BF),
        pltpu.VMEM((ROWS, FF), BF),
        pltpu.VMEM((ROWS, 2 * FF), BF),
        pltpu.VMEM((2 * ROWS, 128), F32),
        pltpu.VMEM((16, 192, TOK), BF),
        pltpu.VMEM((2, 2, 32, 128), BF),
        pltpu.VMEM((2, 96, 2 * D), BF),
        pltpu.VMEM((768, D), BF),
        pltpu.VMEM((2, 2, 256, 2 * FF), BF),
        pltpu.VMEM((2, 2, 512, 2 * FF), BF),
        pltpu.VMEM((2, 2, 192, 512), BF),
        pltpu.VMEM((2, 2, FF, 512), BF),
        dma((30,)), dma((32,)), dma((32,)), dma((32,)),
        dma((10,)), dma((10,)), dma((16,)), dma((16,)),
        dma((16,)), dma((16,)), dma((4,)), dma((4,)),
        dma((16,)), dma((16,)), dma((13,)), dma((2, 4)), dma((2,)),
    ]
    res = pl.pallas_call(
        kernel,
        out_shape=out_shape,
        in_specs=[hbm] * 5,
        out_specs=[hbm] * len(out_shape),
        scratch_shapes=scratch,
        compiler_params=pltpu.CompilerParams(
            collective_id=0, has_side_effects=True, vmem_limit_bytes=63 * 1024 * 1024
        ),
    )(xm, grad_out, w_gate, w_up, w_down)
    return res[:5]


def solution(mesh):
    return jax.shard_map(
        per_device,
        mesh=mesh,
        in_specs=(
            P(("expert", "dp"), None),
            P(("expert", "dp"), None),
            P(("expert", "dp"), None),
            P("expert", "dp", None),
            P("expert", "dp", None),
            P("expert", None, "dp"),
            P(("expert", "dp"), None),
        ),
        out_specs=(
            P(("expert", "dp"), None),
            P(("expert", "dp"), None),
            P("expert", "dp", None),
            P("expert", "dp", None),
            P("expert", None, "dp"),
        ),
        check_vma=False,
    )
```

time: 513 us -> 250 us (0.49); the launches traced: 504 us -> 249 us
  Pallas kernels: 0 us -> 236 us
  waiting for transfers between devices: 222 us -> 0 us
  local copies, waits for them, and re-layouts: 120 us -> 7.74 us
  matrix products: 69.4 us -> 0 us
  other arithmetic: 54.4 us -> 4.67 us
  starting transfers between devices: 23.3 us -> 0 us
  between operations: 14.7 us -> 0.66 us
    pallas_call x0 -> x1, Pallas kernels: none -> 236 us  [per_device(): pl.pallas_call(kernel, out_shape=out_shape, in_specs=[hbm] * 5, out_specs...]
    all_to_all x4 -> x0, waiting for transfers between devices: 220 us -> none  [the longest x1 70.1 us: per_device(): lax.all_to_all(send_x, 'expert', split_axis=0, concat_axis=2, tiled=True)]
    dot_general x9 -> x0, matrix products: 69.4 us -> none  [the longest x1 10.8 us: per_device(): jnp.einsum('lrm,lfm->lrf', dy_in, full_down, preferred_element_type=jnp.f...]
    reshape x3 -> x0, local copies, waits for them, and re-layouts: 37.6 us -> none  [the longest x1 18.8 us: per_device(): pair_dx.reshape(1, local, groups * cap, width)]
    all_to_all x4 -> x0, local copies, waits for them, and re-layouts: 29.7 us -> none  [the longest x1 8.36 us: per_device(): lax.all_to_all(pair_dx.reshape(1, local, groups * cap, width), 'expert',...]
    gather x2 -> x0, local copies, waits for them, and re-layouts: 25.1 us -> none  [the longest x1 12.7 us: per_device(): picked = back.reshape(experts * cap, width)[pos].reshape(rows, topk, width)]
    scatter x1 -> x0, local copies, waits for them, and re-layouts: 24.4 us -> none  [per_device(): jnp.zeros((experts * cap, width), jnp.bfloat16).at[pos]]
    scatter x1 -> x0, other arithmetic: 24.2 us -> none  [per_device(): jnp.zeros((experts * cap, width), jnp.bfloat16).at[pos].set(pair_grad)]
  transfers between devices with their start and end apart: 10 -> 0, of which waited for: 4 -> 0; matrix products, arithmetic and copies ran while one was open for 45% -> 0% of each run, Pallas kernels for 0% -> 0%
where the time goes in v1:
time: 250 us; the launch traced here: 249 us
  Pallas kernels  236 us (94%)
  local copies, waits for them, and re-layouts  7.74 us (3%)
  other arithmetic  4.67 us (2%)
    pallas_call x1, Pallas kernels, per_device(): pl.pallas_call(kernel, out_shape=out_shape, in_specs=[hbm] * 5, out_specs...  236 us
    unnamed x9, local copies, waits for them, and re-layouts  7.74 us

profile of v1, /device:TPU:0, one launch (start us, length us, event | category | flops | bytes accessed | tf_op | source)
XLA Modules:
  0.0 249.2 jit_solution(13750411634429127076)
XLA Ops:
  0.6 0.7 constant_dynamic-update-slice_fusion.3
  1.3 0.7 constant_dynamic-update-slice_fusion.2
  2.0 0.7 constant_dynamic-update-slice_fusion.1
  2.7 0.7 constant_dynamic-update-slice_fusion
  3.4 1.9 pad_maximum_fusion.xm
  5.3 236.2 %shard_map.110 = (bf16[128,2048]{1,0:T(8,128)(2,1)}, bf16[128,2048]{1,0:T(8,128)(2,1)}, bf16[2,512,384]{2,1,0:T(8,128)(2,1)}, bf16[2,512,384]{2,1,0:T(8,128)(2,1...) custom-call(bf16[128,2176]{1,0:T(8,128)(2,1)} %pad_maximum_fusion.xm, ...), custom_call_target="tpu_custom_call" | custom-call | tf_op jit(solution)/shard_map/pallas_call | solution.py:626
  241.5 0.0 copy-start.1
  241.5 0.0 copy-start
  241.5 2.0 copy.21
  243.5 1.9 copy.22
  245.4 2.1 copy.23
  247.5 0.0 copy-done.1
  247.5 0.9 copy.24
  248.4 0.0 copy-done
  248.4 0.9 copy.25
  (1 shorter events, 0.0 us)
Async XLA Ops:
  241.5 6.0 %copy-start.1 = (bf16[2,512,384]{2,1,0:T(8,128)(2,1)S(1)}, bf16[2,512,384]{2,1,0:T(8,128)(2,1)}, u32[]{:S(2)}) copy-start(bf16[2,512,384]{2,1,0:T(8,128)(2,1)} %get-tuple-element.23) | copy-start | bytes 2359300
  241.5 6.9 %copy-start = (bf16[2,384,512]{2,1,0:T(8,128)(2,1)S(1)}, bf16[2,384,512]{2,1,0:T(8,128)(2,1)}, u32[]{:S(2)}) copy-start(bf16[2,384,512]{2,1,0:T(8,128)(2,1)} %get-tuple-element.24) | copy-start | bytes 2359300

commit v2 on v1

v2 whole, which is shorter than its diff:
```python
import jax
import jax.numpy as jnp
from jax import lax
from jax.experimental import pallas as pl
from jax.experimental.pallas import tpu as pltpu
from jax.sharding import PartitionSpec as P

MESH = pl.DeviceIdType.MESH
BF = jnp.bfloat16
F32 = jnp.float32
D = 2048
FF = 384
TOK = 128
CAP = 24
KEEP = {"S": 6, "P": 6, "Q": 12, "Z": 8}
ROWS = 768
XW = D + 128
PLACES = [
    (0, 0), (0, 1), (0, 3), (1, 0), (3, 0), (0, 2), (2, 0),
    (2, 1), (2, 3), (1, 2), (3, 2), (2, 2),
    (1, 1), (1, 3), (3, 1), (3, 3),
]
NT = (((1,), (1,)), ((), ()))
TN = (((0,), (0,)), ((), ()))
NN = (((1,), (0,)), ((), ()))


def dot(a, b, dims):
    return lax.dot_general(a, b, dims, preferred_element_type=F32)


def kernel(
    tok, g, wgate, wup, wdown, eids, gprob,
    mixed, gtok, ggate, gup, gdown,
    xbuf, gbuf, ysib, qopp, qfull, popp, pfull,
    S, L, Wgu, Wd, YD, H, DAB, PW, P4, MB, MT, YL, RB, zhg, zfg, zhd, zfd, early,
    a_send, a_recv, s_send, s_recv, w_send, w_recv, y_send, y_recv,
    q_send, q_recv, p_send, p_recv, z_send, z_recv, loc, ld, yl_sem, m_send,
):
    me = lax.axis_index("expert")
    z = lax.axis_index("dp")
    c = lax.rem(me, 2)
    x = lax.rem(me // 2, 4)
    y = me // 8
    sib = {"expert": me + 1 - 2 * c}
    zr, zl, zo = lax.rem(z + 1, 4), lax.rem(z + 3, 4), lax.rem(z + 2, 4)

    def pq(dp, dq):
        dx = dp + c * (dq - dp)
        dy = dq + c * (dp - dq)
        return {"expert": (lax.rem(y + dy, 4) * 4 + lax.rem(x + dx, 4)) * 2 + c}

    dev = {"P+": pq(1, 0), "P-": pq(3, 0), "Q+": pq(0, 1), "Q-": pq(0, 3), "S": sib, "Z+": {"dp": zr}, "Z-": {"dp": zl}}

    def slot(dp, dq):
        k0, k1 = PLACES.index((dp, dq)), PLACES.index((dq, dp))
        return k0 + c * (k1 - k0)

    barrier = pltpu.get_barrier_semaphore()
    for d in dev.values():
        pl.semaphore_signal(barrier, inc=1, device_id=d, device_id_type=MESH)

    flying = {}

    def send(src, dst, ssem, rsem, to):
        cp = pltpu.make_async_remote_copy(
            src_ref=src, dst_ref=dst, send_sem=ssem, recv_sem=rsem, device_id=dev[to], device_id_type=MESH
        )
        line = flying.setdefault(to[0], [])
        while len(line) >= KEEP[to[0]]:
            line.pop(0).wait_send()
        cp.start()
        line.append(cp)

    def arrived(dst, ssem, rsem):
        pltpu.make_async_remote_copy(
            src_ref=dst, dst_ref=dst, send_sem=ssem, recv_sem=rsem, device_id=dev["S"], device_id_type=MESH
        ).wait_recv()

    half = pl.ds(pl.multiple_of(c * TOK, TOK), TOK)
    other = pl.ds(pl.multiple_of((1 - c) * TOK, TOK), TOK)
    bufs = (xbuf, gbuf)
    counts = {"a": 0, "m": 0}

    def nxt(name):
        counts[name] += 1
        return counts[name] - 1

    def aidx(dp, dq, k):
        return (dp * 4 + dq) * 2 + k

    def blk(dp, dq, k):
        return bufs[k].at[slot(dp, dq), half, :]

    def push(dp, dq, k, to):
        ddp, ddq = dp, dq
        if to == "P+":
            ddp = (dp + 3) % 4
        elif to == "P-":
            ddp = (dp + 1) % 4
        elif to == "Q+":
            ddq = (dq + 3) % 4
        elif to == "Q-":
            ddq = (dq + 1) % 4
        launch(dp, dq, k, slot(ddp, ddq), a_send, nxt("a"), a_recv.at[aidx(ddp, ddq, k)], to)

    def launch(dp, dq, k, r, ssem, i, rsem, to):
        dst = bufs[k].at[r, half, :]
        if dp or dq:
            send(blk(dp, dq, k), dst, ssem.at[i], rsem, to)
        elif k == 1:
            send(g, dst, ssem.at[i], rsem, to)
        else:
            send(tok, bufs[0].at[r, half, pl.ds(0, D)], ssem.at[i], rsem, to)
            send(MT, bufs[0].at[r, half, pl.ds(D, 128)], m_send.at[counts["m"]], rsem, to)
            counts["m"] += 1

    def push_sib(dp, dq, k):
        i = aidx(dp, dq, k)
        launch(dp, dq, k, slot(dp, dq), s_send, i, s_recv.at[i], "S")

    def take(dp, dq, k):
        i = aidx(dp, dq, k)
        arrived(bufs[k].at[slot(dp, dq), half, :], a_send.at[0], a_recv.at[i])

    def take_sib(dp, dq, k):
        i = aidx(dq, dp, k)
        arrived(bufs[k].at[slot(dp, dq), other, :], s_send.at[0], s_recv.at[i])

    eye = (
        lax.broadcasted_iota(jnp.int32, (TOK, TOK), 0) == lax.broadcasted_iota(jnp.int32, (TOK, TOK), 1)
    ).astype(F32).astype(BF)
    prob_in = gprob[...]
    hi = prob_in.astype(BF)
    mid = (prob_in - hi.astype(F32)).astype(BF)
    low = (prob_in - hi.astype(F32) - mid.astype(F32)).astype(BF)
    turned = [dot(v, eye, TN) for v in (eids[...].astype(F32).astype(BF), hi, mid, low)]
    MT[...] = jnp.concatenate(turned + [jnp.zeros((96, TOK), F32)], axis=0).astype(BF)
    pl.semaphore_wait(barrier, 7)

    def zrows(i):
        return pl.ds(pl.multiple_of(i * 512, 512), 512)

    wsrc = (wgate, wup, wdown)

    def wdst(e, k, i):
        if k == 2:
            return Wd.at[e, i]
        return Wgu.at[e, zrows(i), pl.ds(k * FF, FF)]

    own_w = [
        pltpu.make_async_copy(wsrc[k].at[e], wdst(e, k, z), loc.at[5 + 3 * e + k]) for e in range(2) for k in range(3)
    ]

    def w_own(e, kinds=(0, 1, 2)):
        for k in kinds:
            for j, to in enumerate(("Z+", "Z-")):
                wsend(wsrc[k].at[e], wdst(e, k, z), e * 10 + 3 * j + k, to)

    def wsend(src, dst, i, to):
        send(src, dst, w_send.at[i], w_recv.at[i], to)

    def w_parts(e, i):
        lo = pl.ds(pl.multiple_of(i * 512, 512), 256)
        hi = pl.ds(pl.multiple_of(i * 512 + 256, 256), 256)
        return (Wgu.at[e, lo], Wgu.at[e, hi], Wd.at[e, i, pl.ds(0, 192)], Wd.at[e, i, pl.ds(192, 192)])

    def w_fwd(e):
        for k in range(3):
            arrived(wdst(e, k, zl), w_send.at[0], w_recv.at[e * 10 + k])
            arrived(wdst(e, k, zr), w_send.at[0], w_recv.at[e * 10 + 3 + k])
        for j in range(4):
            part = w_parts(e, (zl, zr)[j % 2])[j]
            wsend(part, part, e * 10 + 6 + j, ("Z+", "Z-")[j % 2])

    def w_last(e):
        for j in range(4):
            arrived(w_parts(e, zo)[j], w_send.at[0], w_recv.at[e * 10 + 6 + j])

    for k in range(2):
        push(0, 0, k, "P+")
        push(0, 0, 1 - k, "P-")
        push(0, 0, k, "Q+")
        push(0, 0, 1 - k, "Q-")
        if k == 0:
            w_own(0)
            w_own(1, (0,))
    push_sib(0, 0, 0)
    push_sib(0, 0, 1)
    for cp in own_w:
        cp.start()

    tri = (
        lax.broadcasted_iota(jnp.int32, (TOK, TOK), 0) <= lax.broadcasted_iota(jnp.int32, (TOK, TOK), 1)
    ).astype(F32).astype(BF)
    row8 = lax.broadcasted_iota(jnp.int32, (8, TOK), 0)
    slot_row = lax.broadcasted_iota(jnp.int32, (2 * CAP, TOK), 0).astype(F32)
    cf = c.astype(F32)
    e_own = (2 * me).astype(F32)
    e_sib = (2 * (me + 1 - 2 * c)).astype(F32)

    def load(chip, b, buf):
        r = 0 if chip == (0, 0) else slot(*chip)
        for cp in load_copies(r, b, buf):
            cp.start()

    def load_copies(r, b, buf):
        if isinstance(r, int):
            r0 = b * 512
            mine, theirs = pl.ds(pl.multiple_of(r0 + c * TOK, TOK), TOK), pl.ds(pl.multiple_of(r0 + TOK - c * TOK, TOK), TOK)
            mine_g = pl.ds(pl.multiple_of(r0 + 256 + c * TOK, TOK), TOK)
            theirs_g = pl.ds(pl.multiple_of(r0 + 256 + TOK - c * TOK, TOK), TOK)
            few = pl.ds(pl.multiple_of((1 - c) * TOK, TOK), 32)
            return (
                pltpu.make_async_copy(tok, buf.at[mine, :], ld.at[b, 0]),
                pltpu.make_async_copy(xbuf.at[0, other, pl.ds(0, D)], buf.at[theirs, :], ld.at[b, 1]),
                pltpu.make_async_copy(g, buf.at[mine_g, :], ld.at[b, 2]),
                pltpu.make_async_copy(gbuf.at[0, other, :], buf.at[theirs_g, :], ld.at[b, 3]),
                pltpu.make_async_copy(MT.at[pl.ds(0, 32), :], MB.at[b, c], ld.at[b, 4]),
                pltpu.make_async_copy(xbuf.at[0, few, pl.ds(D, 128)], MB.at[b, 1 - c], ld.at[b, 5]),
            )
        return (
            pltpu.make_async_copy(xbuf.at[r, :, pl.ds(0, D)], buf.at[pl.ds(b * 512, 256), :], ld.at[b, 0]),
            pltpu.make_async_copy(gbuf.at[r], buf.at[pl.ds(b * 512 + 256, 256), :], ld.at[b, 1]),
            pltpu.make_async_copy(xbuf.at[r, pl.ds(0, 32), pl.ds(D, 128)], MB.at[b, 0], ld.at[b, 2]),
            pltpu.make_async_copy(xbuf.at[r, pl.ds(TOK, 32), pl.ds(D, 128)], MB.at[b, 1], ld.at[b, 3]),
        )

    def pick(chip, b, buf):
        r = 0 if chip == (0, 0) else slot(*chip)
        for cp in load_copies(r, b, buf):
            cp.wait()
        ids, prob = [], []
        for t in range(2):
            ids.append(MB[b, t, 0:8].astype(F32))
            prob.append(
                MB[b, t, 8:16].astype(F32) + (MB[b, t, 16:24].astype(F32) + MB[b, t, 24:32].astype(F32))
            )
        ids_c = jnp.where(c == 0, ids[0], ids[1])
        todo = [(ids[0], e_own), (ids[1], e_own), (ids[0], e_own + 1), (ids[1], e_own + 1), (ids_c, e_sib), (ids_c, e_sib + 1)]
        hit = jnp.zeros((8, TOK), F32)
        pv = []
        for j, (idv, e) in enumerate(todo):
            m = jnp.where(idv == e, 1.0, 0.0)
            if j < 4:
                pv.append(jnp.sum(m * prob[j % 2], axis=0, keepdims=True))
            hit = jnp.where(row8 == j, jnp.sum(m, axis=0, keepdims=True), hit)
        rank = dot(hit.astype(BF), tri, NN)
        key = jnp.where(hit > 0.5, rank - 1.0, -1000.0)
        p256, pown, psib = [], [], []
        for e in range(2):
            p0 = jnp.where(key[2 * e : 2 * e + 1] == slot_row, 1.0, 0.0)
            p1 = jnp.where(key[2 * e + 1 : 2 * e + 2] + CAP == slot_row, 1.0, 0.0)
            w = jnp.sum(p0 * pv[2 * e] + p1 * pv[2 * e + 1], axis=1, keepdims=True)
            at = pl.ds(pl.multiple_of(e * ROWS + r * 48, 16), 48)
            PW[at, :] = jnp.broadcast_to(w, (48, 128))
            p256.append(jnp.concatenate([p0, p1], axis=1))
            pown.append(jnp.where(c == 0, p0, p1))
            psib.append(jnp.where(key[4 + e : 5 + e] + CAP * cf == slot_row, 1.0, 0.0))
        P4[r] = jnp.concatenate(pown + psib, axis=0).astype(BF)
        pick_m = jnp.concatenate(p256, axis=0).astype(BF)

        def cols(n, _):
            cc = pl.ds(pl.multiple_of(n * 1024, 1024), 1024)
            for t in range(2):
                src = buf[pl.ds(b * 512 + t * 256, 256), cc]
                got = dot(pick_m, src, NN).astype(BF)
                for e in range(2):
                    at = pl.ds(pl.multiple_of(t * 2 * ROWS + e * ROWS + r * 48, 16), 48)
                    S[at, cc] = got[e * 48 : e * 48 + 48]
            return 0

        lax.fori_loop(0, 2, cols, 0)

    def picks(some, buf):
        for i, chip in enumerate(some):
            for j in (i, i + 1):
                if j < len(some) and (j > i or i == 0):
                    for k in range(2):
                        take_sib(*some[j], k)
                    load(some[j], j % 2, buf)
            pick(chip, i % 2, buf)

    def forward(e, tile):
        first, n = tile
        lo, cnt = first * 48, n * 48
        xs = S[e * ROWS + lo : e * ROWS + lo + cnt, :]
        ab = dot(xs, Wgu[e], NN)
        g0 = (2 + e) * ROWS + lo
        dh = dot(S[g0 : g0 + cnt, 0:512], Wd[e, 0], NT)
        for i in range(1, 4):
            dh = dh + dot(S[g0 : g0 + cnt, i * 512 : i * 512 + 512], Wd[e, i], NT)
        w = PW[e * ROWS + lo : e * ROWS + lo + cnt, 0:1]
        a, b = ab[:, :FF], ab[:, FF:]
        s = 1.0 / (1.0 + jnp.exp(-a))
        act = a * s
        dh = dh * w
        H[e, lo : lo + cnt, :] = (act * b * w).astype(BF)
        DAB[e, lo : lo + cnt, 0:FF] = (dh * b * s * (1.0 + a * (1.0 - s))).astype(BF)
        DAB[e, lo : lo + cnt, FF:] = (dh * act).astype(BF)

    def outputs(e, tile):
        first, n = tile
        lo, cnt = first * 48, n * 48
        for i in range(4):
            yv = dot(H[e, lo : lo + cnt, :], Wd[e, i], NN).astype(BF)
            YD[first : first + n, e * 48 : e * 48 + 48, i * 512 : i * 512 + 512] = yv.reshape(n, 48, 512)
        for i in range(4):
            dv = dot(DAB[e, lo : lo + cnt, :], Wgu[e, i * 512 : i * 512 + 512, :], NT).astype(BF)
            YD[first : first + n, e * 48 : e * 48 + 48, D + i * 512 : D + i * 512 + 512] = dv.reshape(n, 48, 512)

    def weight_grads(e):
        def part(j, _):
            i = lax.rem(z + j, 4)
            cc = zrows(i)
            xs = S[e * ROWS : e * ROWS + ROWS, cc]
            gs = S[(2 + e) * ROWS : (3 + e) * ROWS, cc]
            Wgu[e, cc, :] = dot(xs, DAB[e], TN).astype(BF)
            Wd[e, i] = dot(H[e], gs, TN).astype(BF)
            return 0

        lax.fori_loop(2, 3, part, 0)
        z_first(e)
        lax.fori_loop(3, 6, part, 0)

    def zsend(src, dst, i, to):
        send(src, dst, z_send.at[i], z_recv.at[i], to)

    def z_first(e):
        base = e * 8
        lo = pl.ds(pl.multiple_of(zo * 512, 512), 256)
        hi = pl.ds(pl.multiple_of(zo * 512 + 256, 256), 256)
        zsend(Wgu.at[e, lo], zhg.at[e, 0], base + 0, "Z+")
        zsend(Wgu.at[e, hi], zhg.at[e, 1], base + 1, "Z-")
        zsend(Wd.at[e, zo, pl.ds(0, 192)], zhd.at[e, 0], base + 2, "Z+")
        zsend(Wd.at[e, zo, pl.ds(192, 192)], zhd.at[e, 1], base + 3, "Z-")

    def z_second(e):
        base = e * 8
        for i, (dst, rows) in enumerate(((zhg.at[e, 0], 0), (zhg.at[e, 1], 0), (zhd.at[e, 0], 0), (zhd.at[e, 1], 0))):
            arrived(dst, z_send.at[0], z_recv.at[base + i])

        def add(j, _):
            for i, (zz, off) in enumerate(((zr, 0), (zl, 256))):
                at = pl.ds(pl.multiple_of(zz * 512 + off + j * 32, 32), 32)
                Wgu[e, at, :] = (Wgu[e, at, :].astype(F32) + zhg[e, i, pl.ds(j * 32, 32), :].astype(F32)).astype(BF)
            return 0

        lax.fori_loop(0, 8, add, 0)

        def add_d(j, _):
            for i, (zz, off) in enumerate(((zr, 0), (zl, 192))):
                at = pl.ds(pl.multiple_of(off + j * 32, 32), 32)
                Wd[e, zz, at, :] = (Wd[e, zz, at, :].astype(F32) + zhd[e, i, pl.ds(j * 32, 32), :].astype(F32)).astype(BF)
            return 0

        lax.fori_loop(0, 6, add_d, 0)
        zsend(Wgu.at[e, zrows(zr)], zfg.at[e, 0], base + 4, "Z+")
        zsend(Wgu.at[e, zrows(zl)], zfg.at[e, 1], base + 5, "Z-")
        zsend(Wd.at[e, zr], zfd.at[e, 0], base + 6, "Z+")
        zsend(Wd.at[e, zl], zfd.at[e, 1], base + 7, "Z-")

    outs = []

    def z_third(e):
        base = e * 8
        for i, dst in enumerate((zfg.at[e, 0], zfg.at[e, 1], zfd.at[e, 0], zfd.at[e, 1])):
            arrived(dst, z_send.at[0], z_recv.at[base + 4 + i])

        def add(j, _):
            at = pl.ds(pl.multiple_of(z * 512 + j * 32, 32), 32)
            jj = pl.ds(pl.multiple_of(j * 32, 32), 32)
            Wgu[e, at, :] = (
                Wgu[e, at, :].astype(F32) + zfg[e, 0, jj, :].astype(F32) + zfg[e, 1, jj, :].astype(F32)
            ).astype(BF)
            return 0

        lax.fori_loop(0, 16, add, 0)

        def add_d(j, _):
            jj = pl.ds(pl.multiple_of(j * 32, 32), 32)
            Wd[e, z, jj, :] = (
                Wd[e, z, jj, :].astype(F32) + zfd[e, 0, jj, :].astype(F32) + zfd[e, 1, jj, :].astype(F32)
            ).astype(BF)
            return 0

        lax.fori_loop(0, 12, add_d, 0)
        for i, cp in enumerate(
            (
                (Wgu.at[e, zrows(z), pl.ds(0, FF)], ggate.at[e]),
                (Wgu.at[e, zrows(z), pl.ds(FF, FF)], gup.at[e]),
                (Wd.at[e, z], gdown.at[e]),
            )
        ):
            cp = pltpu.make_async_copy(cp[0], cp[1], loc.at[5 + e * 3 + i])
            cp.start()
            outs.append(cp)

    far = [(2, 2), (1, 2), (3, 2), (0, 2)]
    near = [(2, 1), (2, 3), (0, 1), (0, 3), (1, 1), (1, 3), (3, 1), (3, 3)]
    mine = [(2, 0), (1, 0), (3, 0), (0, 0)]
    chips = far + near + mine

    def yd_sends(some):
        for i, (dp, dq) in enumerate(chips):
            if (dp, dq) in some:
                r = slot(dq, dp)
                send(YD.at[r], ysib.at[r], y_send.at[i], y_recv.at[i], "S")

    def yd_load(i):
        r = slot(*chips[i])
        return pltpu.make_async_copy(ysib.at[r], YL.at[i % 2], yl_sem.at[i % 2])

    def yd_start(i):
        r = slot(*chips[i])
        arrived(ysib.at[r], y_send.at[0], y_recv.at[i])
        yd_load(i).start()

    def cblk(dp, dq, k=0, n=1):
        if dq == 2:
            return L, dp * 256 + k * 128, n * 128
        if dp in (0, 2) and dq:
            return early, dp * 256 + dq // 2 * 256 + k * 128, n * 128
        return S, dp * 768 + {0: 0, 1: 256, 3: 512}[dq] + k * 128, n * 128

    def cref(dp, dq, k=0, n=1):
        ref, row, cnt = cblk(dp, dq, k, n)
        return ref.at[pl.ds(row, cnt), :]

    def combine(dp, dq, ahead=True):
        i = chips.index((dp, dq))
        if i + 1 < 16 and ahead:
            yd_start(i + 1)
        yd_load(i).wait()
        r = slot(dp, dq)
        ref, row, _ = cblk(dp, dq)
        pm = P4[r]

        def cols(n, _):
            cc = pl.ds(pl.multiple_of(n * 512, 512), 512)
            for k in range(2):
                ck = pl.ds(pl.multiple_of(k * D + n * 512, 512), 512)
                rows = jnp.concatenate([YD[r, :, ck], YL[i % 2, :, ck]], axis=0)
                ref[row + k * 128 : row + k * 128 + 128, cc] = dot(pm, rows, TN).astype(BF)
            return 0

        lax.fori_loop(0, 4, cols, 0)

    def fetch(pairs):
        cps = [pltpu.make_async_copy(s, d, ld.at[0, i]) for i, (s, d) in enumerate(pairs)]
        for cp in cps:
            cp.start()
        for cp in cps:
            cp.wait()

    def accumulate(dp, dq, k, n, parts):
        ref, row, cnt = cblk(dp, dq, k, n)

        def add(j, _):
            at = pl.ds(pl.multiple_of(row + j * 16, 16), 16)
            total = ref[at, :].astype(F32)
            for off in parts:
                total = total + RB[pl.ds(pl.multiple_of(off + j * 16, 16), 16), :].astype(F32)
            ref[at, :] = total.astype(BF)
            return 0

        lax.fori_loop(0, cnt // 16, add, 0)

    def qsend(src, dst, dp, j, to):
        send(src, dst, q_send.at[dp * 4 + j], q_recv.at[dp * 4 + j], to)

    def q_first(dp):
        qsend(cref(dp, 2, 0), qopp.at[dp, 0], dp, 0, "Q+")
        qsend(cref(dp, 2, 1), qopp.at[dp, 1], dp, 1, "Q-")

    def q_second(dp):
        arrived(qopp.at[dp, 0], q_send.at[0], q_recv.at[dp * 4 + 0])
        arrived(qopp.at[dp, 1], q_send.at[0], q_recv.at[dp * 4 + 1])
        fetch([(qopp.at[dp, 0], RB.at[pl.ds(512, 128)]), (qopp.at[dp, 1], RB.at[pl.ds(640, 128)])])
        accumulate(dp, 1, 0, 1, (512,))
        qsend(cref(dp, 1, 0, 2), qfull.at[dp, 0], dp, 2, "Q+")
        accumulate(dp, 3, 1, 1, (640,))
        qsend(cref(dp, 3, 0, 2), qfull.at[dp, 1], dp, 3, "Q-")

    def psend(src, dst, j, to):
        send(src, dst, p_send.at[j], p_recv.at[j], to)

    def q_third(dp):
        arrived(qfull.at[dp, 0], q_send.at[0], q_recv.at[dp * 4 + 2])
        arrived(qfull.at[dp, 1], q_send.at[0], q_recv.at[dp * 4 + 3])
        fetch([(qfull.at[dp, 0], RB.at[pl.ds(0, 256)]), (qfull.at[dp, 1], RB.at[pl.ds(256, 256)])])
        accumulate(dp, 0, 0, 2, (0, 256))
        if dp == 2:
            psend(cref(2, 0, 0), popp.at[0], 0, "P+")
            psend(cref(2, 0, 1), popp.at[1], 1, "P-")
        elif dp == 1:
            arrived(popp.at[0], p_send.at[0], p_recv.at[0])
            fetch([(popp.at[0], RB.at[pl.ds(512, 128)])])
            accumulate(1, 0, 0, 1, (512,))
            psend(cref(1, 0, 0, 2), pfull.at[0], 2, "P+")
        elif dp == 3:
            arrived(popp.at[1], p_send.at[0], p_recv.at[1])
            fetch([(popp.at[1], RB.at[pl.ds(512, 128)])])
            accumulate(3, 0, 1, 1, (512,))
            psend(cref(3, 0, 0, 2), pfull.at[1], 3, "P-")
        else:
            arrived(pfull.at[0], p_send.at[0], p_recv.at[2])
            arrived(pfull.at[1], p_send.at[0], p_recv.at[3])
            fetch([(pfull.at[0], RB.at[pl.ds(0, 256)]), (pfull.at[1], RB.at[pl.ds(256, 256)])])
            accumulate(0, 0, 0, 2, (0, 256))
            for k, out in enumerate((mixed, gtok)):
                cp = pltpu.make_async_copy(cref(0, 0, k), out, loc.at[11 + k])
                cp.start()
                outs.append(cp)

    T0, T1, T2 = (0, 7), (7, 5), (12, 4)
    take(3, 0, 0)
    push(3, 0, 0, "P+")
    take(1, 0, 1)
    push(1, 0, 1, "P-")
    take(0, 3, 0)
    push(0, 3, 0, "Q+")
    take(0, 1, 1)
    push(0, 1, 1, "Q-")
    push(3, 0, 0, "Q+")
    push(1, 0, 1, "Q-")
    take(1, 0, 0)
    push(1, 0, 0, "Q+")
    take(3, 0, 1)
    push(3, 0, 1, "Q-")
    take(0, 1, 0)
    take(0, 3, 1)
    for chip in ((1, 0), (3, 0), (0, 1), (0, 3)):
        for k in range(2):
            push_sib(*chip, k)
    w_fwd(0)
    w_own(1, (1, 2))
    picks([(0, 0)], L)
    for k in range(2):
        take(2, 0, k)
    push(2, 0, 0, "Q+")
    push(2, 0, 1, "Q-")
    push(2, 0, 0, "Q-")
    push(2, 0, 1, "Q+")
    for k in range(2):
        push_sib(2, 0, k)
        take(0, 2, k)
        push_sib(0, 2, k)
    picks([(0, 1), (0, 3), (1, 0), (3, 0)], L)
    for dp in (3, 1):
        take(dp, 3, 0)
        push(dp, 3, 0, "Q+")
        take(dp, 1, 1)
        push(dp, 1, 1, "Q-")
    for dp in (3, 1):
        push_sib(dp, 3, 0)
        push_sib(dp, 1, 1)
    picks([(0, 2), (2, 0)], L)
    take(2, 3, 0)
    push(2, 3, 0, "Q+")
    take(2, 1, 1)
    push(2, 1, 1, "Q-")
    for dp in (3, 1):
        push(dp, 0, 0, "Q-")
        push(dp, 0, 1, "Q+")
    take(2, 1, 0)
    take(2, 3, 1)
    for chip in ((2, 1), (2, 3)):
        for k in range(2):
            push_sib(*chip, k)
    w_last(0)
    for cp in own_w:
        cp.wait()
    forward(0, T0)
    outputs(0, T0)
    for dp in (3, 1):
        for k in range(2):
            take(dp, 2, k)
            push_sib(dp, 2, k)
    w_fwd(1)
    picks([(2, 1), (2, 3), (1, 2), (3, 2)], L)
    for k in range(2):
        take(2, 2, k)
        push_sib(2, 2, k)
    picks([(2, 2)], L)
    forward(0, T1)
    outputs(0, T1)
    w_last(1)
    forward(1, T1)
    outputs(1, T1)
    yd_sends([(2, 2), (1, 2), (3, 2), (2, 1), (2, 3)])
    forward(1, T0)
    outputs(1, T0)
    yd_sends([(0, 2), (0, 1), (0, 3), (2, 0), (1, 0), (3, 0), (0, 0)])
    yd_start(0)
    for dp, dq in far:
        combine(dp, dq)
        q_first(dp)
    combine(2, 1)
    combine(2, 3)
    for dp in (3, 1):
        take(dp, 1, 0)
        push_sib(dp, 1, 0)
        take(dp, 3, 1)
        push_sib(dp, 3, 1)
    picks([(1, 1), (1, 3), (3, 1), (3, 3)], RB)
    q_second(2)
    forward(0, T2)
    outputs(0, T2)
    for cp in flying["Z"]:
        cp.wait_send()
    flying["Z"] = []
    weight_grads(0)
    combine(0, 1)
    combine(0, 3, False)
    forward(1, T2)
    outputs(1, T2)
    yd_sends([(1, 1), (1, 3), (3, 1), (3, 3)])
    yd_start(8)
    q_second(0)
    weight_grads(1)
    combine(1, 1)
    combine(1, 3)
    q_second(1)
    z_second(0)
    combine(3, 1)
    combine(3, 3)
    q_second(3)
    z_second(1)
    for dp, dq in mine:
        combine(dp, dq)
    q_third(2)
    q_third(1)
    q_third(3)
    z_third(0)
    q_third(0)
    z_third(1)
    for cp in outs:
        cp.wait()
    for line in flying.values():
        for cp in line:
            cp.wait_send()


def per_device(tokens, expert_ids, gate_prob, w_gate, w_up, w_down, grad_out):
    sds = jax.ShapeDtypeStruct
    hbm = pl.BlockSpec(memory_space=pl.ANY)
    dma = pltpu.SemaphoreType.DMA
    out_shape = (
        sds((TOK, D), BF),
        sds((TOK, D), BF),
        sds((2, 512, FF), BF),
        sds((2, 512, FF), BF),
        sds((2, FF, 512), BF),
        sds((16, 256, XW), BF),
        sds((16, 256, D), BF),
        sds((16, 96, 2 * D), BF),
        sds((4, 2, TOK, D), BF),
        sds((4, 2, 256, D), BF),
        sds((2, TOK, D), BF),
        sds((2, 256, D), BF),
    )
    scratch = [
        pltpu.VMEM((4 * ROWS, D), BF),
        pltpu.VMEM((1024, D), BF),
        pltpu.VMEM((2, D, 2 * FF), BF),
        pltpu.VMEM((2, 4, FF, 512), BF),
        pltpu.VMEM((16, 96, 2 * D), BF),
        pltpu.VMEM((2, ROWS, FF), BF),
        pltpu.VMEM((2, ROWS, 2 * FF), BF),
        pltpu.VMEM((2 * ROWS, 128), F32),
        pltpu.VMEM((16, 192, TOK), BF),
        pltpu.VMEM((2, 2, 32, 128), BF),
        pltpu.VMEM((128, 128), BF),
        pltpu.VMEM((2, 96, 2 * D), BF),
        pltpu.VMEM((1024, D), BF),
        pltpu.VMEM((2, 2, 256, 2 * FF), BF),
        pltpu.VMEM((2, 2, 512, 2 * FF), BF),
        pltpu.VMEM((2, 2, 192, 512), BF),
        pltpu.VMEM((2, 2, FF, 512), BF),
        pltpu.VMEM((1024, D), BF),
        dma((30,)), dma((32,)), dma((32,)), dma((32,)),
        dma((20,)), dma((20,)), dma((16,)), dma((16,)),
        dma((16,)), dma((16,)), dma((4,)), dma((4,)),
        dma((16,)), dma((16,)), dma((13,)), dma((2, 6)), dma((2,)), dma((5,)),
    ]
    res = pl.pallas_call(
        kernel,
        out_shape=out_shape,
        in_specs=[hbm] * 5 + [pl.BlockSpec(memory_space=pltpu.VMEM)] * 2,
        out_specs=[hbm] * len(out_shape),
        scratch_shapes=scratch,
        compiler_params=pltpu.CompilerParams(
            collective_id=0, has_side_effects=True, vmem_limit_bytes=63 * 1024 * 1024
        ),
    )(tokens, grad_out, w_gate, w_up, w_down, expert_ids, gate_prob)
    return res[:5]


def solution(mesh):
    return jax.shard_map(
        per_device,
        mesh=mesh,
        in_specs=(
            P(("expert", "dp"), None),
            P(("expert", "dp"), None),
            P(("expert", "dp"), None),
            P("expert", "dp", None),
            P("expert", "dp", None),
            P("expert", None, "dp"),
            P(("expert", "dp"), None),
        ),
        out_specs=(
            P(("expert", "dp"), None),
            P(("expert", "dp"), None),
            P("expert", "dp", None),
            P("expert", "dp", None),
            P("expert", None, "dp"),
        ),
        check_vma=False,
    )
```

time: 250 us -> 229 us (0.916)
  Pallas kernels: 236 us -> 214 us
  local copies, waits for them, and re-layouts: 7.74 us -> 12.8 us
  other arithmetic: 4.67 us -> 0 us
    pallas_call x1, Pallas kernels: 236 us -> 214 us  [per_device(): pl.pallas_call(kernel, out_shape=out_shape, in_specs=[hbm] * 5 + [pl.Bloc...]
    unnamed x9 -> x7, local copies, waits for them, and re-layouts: 7.74 us -> 12.8 us
    unnamed x4 -> x0, other arithmetic: 2.78 us -> none
where the time goes in v2:
time: 229 us; the launch traced here: 227 us
  Pallas kernels  214 us (93%)
  local copies, waits for them, and re-layouts  12.8 us (6%)
    pallas_call x1, Pallas kernels, per_device(): pl.pallas_call(kernel, out_shape=out_shape, in_specs=[hbm] * 5 + [pl.Bloc...  214 us
    unnamed x7, local copies, waits for them, and re-layouts  12.8 us

profile of v2, /device:TPU:0, one launch (start us, length us, event | category | flops | bytes accessed | tf_op | source)
XLA Modules:
  0.0 227.5 jit_solution(11424769243463717386)
XLA Ops:
  0.6 1.4 copy.12.eids
  2.0 1.4 copy.13.gprob
  3.5 214.0 %shard_map.110 = (bf16[128,2048]{1,0:T(8,128)(2,1)}, bf16[128,2048]{1,0:T(8,128)(2,1)}, bf16[2,512,384]{2,1,0:T(8,128)(2,1)}, bf16[2,512,384]{2,1,0:T(8,128)(2,1...) custom-call(bf16[128,2048]{1,0:T(8,128)(2,1)} %tok.1, ...), custom_call_target="tpu_custom_call" | custom-call | tf_op jit(solution)/shard_map/pallas_call | solution.py:687
  217.5 1.9 copy.19
  219.4 1.9 copy.20
  221.2 2.1 copy.21
  223.3 2.1 copy.22
  225.4 2.1 copy.23

commit v3 on v2

--- a/solution.py
+++ b/solution.py
@@ -31,9 +31,9 @@
 
 def kernel(
     tok, g, wgate, wup, wdown, eids, gprob,
-    mixed, gtok, ggate, gup, gdown,
-    xbuf, gbuf, ysib, qopp, qfull, popp, pfull,
-    S, L, Wgu, Wd, YD, H, DAB, PW, P4, MB, MT, YL, RB, zhg, zfg, zhd, zfd, early,
+    own_r, own_gu, own_d, zfg, zfd, pfull,
+    xbuf, gbuf, ysib, qopp, qfull, popp,
+    S, L, Wgu, Wd, YD, H, DAB, PW, P4, MB, MT, YL, RB, zhg, zhd, early,
     a_send, a_recv, s_send, s_recv, w_send, w_recv, y_send, y_recv,
     q_send, q_recv, p_send, p_recv, z_send, z_recv, loc, ld, yl_sem, m_send,
 ):
@@ -127,15 +127,12 @@
         i = aidx(dq, dp, k)
         arrived(bufs[k].at[slot(dp, dq), other, :], s_send.at[0], s_recv.at[i])
 
-    eye = (
-        lax.broadcasted_iota(jnp.int32, (TOK, TOK), 0) == lax.broadcasted_iota(jnp.int32, (TOK, TOK), 1)
-    ).astype(F32).astype(BF)
     prob_in = gprob[...]
     hi = prob_in.astype(BF)
     mid = (prob_in - hi.astype(F32)).astype(BF)
     low = (prob_in - hi.astype(F32) - mid.astype(F32)).astype(BF)
-    turned = [dot(v, eye, TN) for v in (eids[...].astype(F32).astype(BF), hi, mid, low)]
-    MT[...] = jnp.concatenate(turned + [jnp.zeros((96, TOK), F32)], axis=0).astype(BF)
+    meta = [eids[...].astype(F32), hi.astype(F32), mid.astype(F32), low.astype(F32), jnp.zeros((96, TOK), F32)]
+    MT[...] = jnp.concatenate(meta, axis=0).astype(BF)
     pl.semaphore_wait(barrier, 7)
 
     def zrows(i):
@@ -367,32 +364,9 @@
         for i, dst in enumerate((zfg.at[e, 0], zfg.at[e, 1], zfd.at[e, 0], zfd.at[e, 1])):
             arrived(dst, z_send.at[0], z_recv.at[base + 4 + i])
 
-        def add(j, _):
-            at = pl.ds(pl.multiple_of(z * 512 + j * 32, 32), 32)
-            jj = pl.ds(pl.multiple_of(j * 32, 32), 32)
-            Wgu[e, at, :] = (
-                Wgu[e, at, :].astype(F32) + zfg[e, 0, jj, :].astype(F32) + zfg[e, 1, jj, :].astype(F32)
-            ).astype(BF)
-            return 0
-
-        lax.fori_loop(0, 16, add, 0)
-
-        def add_d(j, _):
-            jj = pl.ds(pl.multiple_of(j * 32, 32), 32)
-            Wd[e, z, jj, :] = (
-                Wd[e, z, jj, :].astype(F32) + zfd[e, 0, jj, :].astype(F32) + zfd[e, 1, jj, :].astype(F32)
-            ).astype(BF)
-            return 0
-
-        lax.fori_loop(0, 12, add_d, 0)
-        for i, cp in enumerate(
-            (
-                (Wgu.at[e, zrows(z), pl.ds(0, FF)], ggate.at[e]),
-                (Wgu.at[e, zrows(z), pl.ds(FF, FF)], gup.at[e]),
-                (Wd.at[e, z], gdown.at[e]),
-            )
-        ):
-            cp = pltpu.make_async_copy(cp[0], cp[1], loc.at[5 + e * 3 + i])
+    def z_own(e):
+        for i, (src, dst) in enumerate(((Wgu.at[e, zrows(z)], own_gu.at[e]), (Wd.at[e, z], own_d.at[e]))):
+            cp = pltpu.make_async_copy(src, dst, loc.at[e * 2 + i])
             cp.start()
             outs.append(cp)
 
@@ -504,14 +478,11 @@
             accumulate(3, 0, 1, 1, (512,))
             psend(cref(3, 0, 0, 2), pfull.at[1], 3, "P-")
         else:
+            cp = pltpu.make_async_copy(cref(0, 0, 0, 2), own_r, loc.at[4])
+            cp.start()
+            outs.append(cp)
             arrived(pfull.at[0], p_send.at[0], p_recv.at[2])
             arrived(pfull.at[1], p_send.at[0], p_recv.at[3])
-            fetch([(pfull.at[0], RB.at[pl.ds(0, 256)]), (pfull.at[1], RB.at[pl.ds(256, 256)])])
-            accumulate(0, 0, 0, 2, (0, 256))
-            for k, out in enumerate((mixed, gtok)):
-                cp = pltpu.make_async_copy(cref(0, 0, k), out, loc.at[11 + k])
-                cp.start()
-                outs.append(cp)
 
     T0, T1, T2 = (0, 7), (7, 5), (12, 4)
     take(3, 0, 0)
@@ -619,6 +590,8 @@
     yd_start(8)
     q_second(0)
     weight_grads(1)
+    z_own(0)
+    z_own(1)
     combine(1, 1)
     combine(1, 3)
     q_second(1)
@@ -642,23 +615,33 @@
             cp.wait_send()
 
 
+def finish(own_r, own_gu, own_d, zfg, zfd, pfull, mixed, gtok, ggate, gup, gdown):
+    for k, out in enumerate((mixed, gtok)):
+        out[...] = (own_r[k].astype(F32) + pfull[0, k].astype(F32) + pfull[1, k].astype(F32)).astype(BF)
+    for e in range(2):
+        gu = (own_gu[e].astype(F32) + zfg[e, 0].astype(F32) + zfg[e, 1].astype(F32)).astype(BF)
+        ggate[e] = gu[:, :FF]
+        gup[e] = gu[:, FF:]
+        gdown[e] = (own_d[e].astype(F32) + zfd[e, 0].astype(F32) + zfd[e, 1].astype(F32)).astype(BF)
+
+
 def per_device(tokens, expert_ids, gate_prob, w_gate, w_up, w_down, grad_out):
     sds = jax.ShapeDtypeStruct
     hbm = pl.BlockSpec(memory_space=pl.ANY)
     dma = pltpu.SemaphoreType.DMA
     out_shape = (
-        sds((TOK, D), BF),
-        sds((TOK, D), BF),
-        sds((2, 512, FF), BF),
-        sds((2, 512, FF), BF),
+        sds((256, D), BF),
+        sds((2, 512, 2 * FF), BF),
         sds((2, FF, 512), BF),
+        sds((2, 2, 512, 2 * FF), BF),
+        sds((2, 2, FF, 512), BF),
+        sds((2, 256, D), BF),
         sds((16, 256, XW), BF),
         sds((16, 256, D), BF),
         sds((16, 96, 2 * D), BF),
         sds((4, 2, TOK, D), BF),
         sds((4, 2, 256, D), BF),
         sds((2, TOK, D), BF),
-        sds((2, 256, D), BF),
     )
     scratch = [
         pltpu.VMEM((4 * ROWS, D), BF),
@@ -675,9 +658,7 @@
         pltpu.VMEM((2, 96, 2 * D), BF),
         pltpu.VMEM((1024, D), BF),
         pltpu.VMEM((2, 2, 256, 2 * FF), BF),
-        pltpu.VMEM((2, 2, 512, 2 * FF), BF),
         pltpu.VMEM((2, 2, 192, 512), BF),
-        pltpu.VMEM((2, 2, FF, 512), BF),
         pltpu.VMEM((1024, D), BF),
         dma((30,)), dma((32,)), dma((32,)), dma((32,)),
         dma((20,)), dma((20,)), dma((16,)), dma((16,)),
@@ -693,8 +674,35 @@
         compiler_params=pltpu.CompilerParams(
             collective_id=0, has_side_effects=True, vmem_limit_bytes=63 * 1024 * 1024
         ),
-    )(tokens, grad_out, w_gate, w_up, w_down, expert_ids, gate_prob)
-    return res[:5]
+    )(tokens, grad_out, w_gate, w_up, w_down, expert_ids.T, gate_prob.T)
+    block = pl.BlockSpec
+    return pl.pallas_call(
+        finish,
+        grid=(4,),
+        out_shape=(
+            sds((TOK, D), BF),
+            sds((TOK, D), BF),
+            sds((2, 512, FF), BF),
+            sds((2, 512, FF), BF),
+            sds((2, FF, 512), BF),
+        ),
+        in_specs=[
+            block((2, 32, D), lambda i: (0, i, 0)),
+            block((2, 128, 2 * FF), lambda i: (0, i, 0)),
+            block((2, 96, 512), lambda i: (0, i, 0)),
+            block((2, 2, 128, 2 * FF), lambda i: (0, 0, i, 0)),
+            block((2, 2, 96, 512), lambda i: (0, 0, i, 0)),
+            block((2, 2, 32, D), lambda i: (0, 0, i, 0)),
+        ],
+        out_specs=(
+            block((32, D), lambda i: (i, 0)),
+            block((32, D), lambda i: (i, 0)),
+            block((2, 128, FF), lambda i: (0, i, 0)),
+            block((2, 128, FF), lambda i: (0, i, 0)),
+            block((2, 96, 512), lambda i: (0, i, 0)),
+        ),
+        compiler_params=pltpu.CompilerParams(vmem_limit_bytes=63 * 1024 * 1024),
+    )(res[0].reshape(2, TOK, D), *res[1:5], res[5].reshape(2, 2, TOK, D))
 
 
 def solution(mesh):

time: 229 us -> 221 us (0.965)
  local copies, waits for them, and re-layouts: 12.8 us -> 0 us
  Pallas kernels: 214 us -> 219 us
    unnamed x7 -> x0, local copies, waits for them, and re-layouts: 12.8 us -> none
    pallas_call x0 -> x1, Pallas kernels: none -> 6.17 us  [per_device(): pl.pallas_call(finish, grid=(4,), out_shape=(sds((TOK, D), BF), sds((TOK,...]
where the time goes in v3:
time: 221 us; the launch traced here: 219 us
  Pallas kernels  219 us (99%)
    pallas_call x1, Pallas kernels, per_device(): pl.pallas_call(kernel, out_shape=out_shape, in_specs=[hbm] * 5 + [pl.Bloc...  212 us
    pallas_call x1, Pallas kernels, per_device(): pl.pallas_call(finish, grid=(4,), out_shape=(sds((TOK, D), BF), sds((TOK,...  6.17 us

profile of v3, /device:TPU:0, one launch (start us, length us, event | category | flops | bytes accessed | tf_op | source)
XLA Modules:
  0.0 219.3 jit_solution(3204651340043268594)
XLA Ops:
  0.6 212.4 %shard_map.110 = (bf16[256,2048]{1,0:T(8,128)(2,1)}, bf16[2,512,768]{2,1,0:T(8,128)(2,1)}, bf16[2,384,512]{2,1,0:T(8,128)(2,1)}, bf16[2,2,512,768]{3,2,1,0:T(8,1...) custom-call(bf16[128,2048]{1,0:T(8,128)(2,1)} %tok.1, ...), custom_call_target="tpu_custom_call" | custom-call | tf_op jit(solution)/shard_map/pallas_call | solution.py:668
  213.1 6.2 %shard_map.111 = (bf16[128,2048]{1,0:T(8,128)(2,1)}, bf16[128,2048]{1,0:T(8,128)(2,1)}, bf16[2,512,384]{2,1,0:T(8,128)(2,1)}, bf16[2,512,384]{2,1,0:T(8,128)(2,1)}, bf16[2,384,512]{2,1,0:T(8,128)(2,1)}) custom-call(bf16[2,128,2048]{2,1,0:T(8,128)(2,1)} %bitcast.5, bf16[2,512,768]{2,1,0:T(8,128)(2,1)} %get-tuple-element.12.own_gu, ...), custom_call_target="tpu_custom_call" | custom-call | tf_op jit(solution)/shard_map/pallas_call | solution.py:679

commit v4 on v3

--- a/solution.py
+++ b/solution.py
@@ -600,9 +600,10 @@
     combine(3, 3)
     q_second(3)
     z_second(1)
-    for dp, dq in mine:
+    combine(2, 0)
+    q_third(2)
+    for dp, dq in mine[1:]:
         combine(dp, dq)
-    q_third(2)
     q_third(1)
     q_third(3)
     z_third(0)

time: 221 us -> 221 us (level)
  no operation moved by 1% of the time
where the time goes in v4:
time: 221 us; the launch traced here: 219 us
  Pallas kernels  219 us (99%)
    pallas_call x1, Pallas kernels, per_device(): pl.pallas_call(kernel, out_shape=out_shape, in_specs=[hbm] * 5 + [pl.Bloc...  212 us
    pallas_call x1, Pallas kernels, per_device(): pl.pallas_call(finish, grid=(4,), out_shape=(sds((TOK, D), BF), sds((TOK,...  6.17 us

profile of v4, /device:TPU:0, one launch (start us, length us, event | category | flops | bytes accessed | tf_op | source)
XLA Modules:
  0.0 219.3 jit_solution(16355057000329793921)
XLA Ops:
  0.6 212.4 %shard_map.110 = (bf16[256,2048]{1,0:T(8,128)(2,1)}, bf16[2,512,768]{2,1,0:T(8,128)(2,1)}, bf16[2,384,512]{2,1,0:T(8,128)(2,1)}, bf16[2,2,512,768]{3,2,1,0:T(8,1...) custom-call(bf16[128,2048]{1,0:T(8,128)(2,1)} %tok.1, ...), custom_call_target="tpu_custom_call" | custom-call | tf_op jit(solution)/shard_map/pallas_call | solution.py:669
  213.1 6.2 %shard_map.111 = (bf16[128,2048]{1,0:T(8,128)(2,1)}, bf16[128,2048]{1,0:T(8,128)(2,1)}, bf16[2,512,384]{2,1,0:T(8,128)(2,1)}, bf16[2,512,384]{2,1,0:T(8,128)(2,1)}, bf16[2,384,512]{2,1,0:T(8,128)(2,1)}) custom-call(bf16[2,128,2048]{2,1,0:T(8,128)(2,1)} %bitcast.5, bf16[2,512,768]{2,1,0:T(8,128)(2,1)} %get-tuple-element.12.own_gu, ...), custom_call_target="tpu_custom_call" | custom-call | tf_op jit(solution)/shard_map/pallas_call | solution.py:680
